TPU v7x, 32 devices: a whole 2x2x4 slice. The times are simulated.
32 devices in a mesh: rep: 2 (over x), ad: 16 (over z, y, core).
Axes of the slice: x: 2, y: 2, z: 4, core: 2. Of those that a mesh axis runs over, the one named last changes fastest.
Arguments:
- tokens: bfloat16 [16384, 8192], P(('rep', 'ad')), parts along dimension 0, may hold values from -6 to 6
- value_weight: bfloat16 [8192, 1024], P('ad'), may hold values from -0.0625 to 0.0625
- down_weight: bfloat16 [64, 8192, 64], P('ad'), may hold values from -0.0625 to 0.0625
- up_weight: bfloat16 [64, 64, 1024], P('ad'), may hold values from -0.75 to 0.75
- request_adapter: int32 [16384], P(('rep', 'ad')), parts along dimension 0, may hold values from 0 to 63, as said below
- adapter_home_slot: int32 [128], P('rep'), parts along dimension 0, may hold values from 0 to 63, as said below
Outputs:
- adapted: bfloat16 [16384, 1024], P(('rep', 'ad')), parts along dimension 0
There are 2 independent parts, one for each index of `rep`. A program takes and returns all parts, laid end to end along the dimension named above; an argument that names none is the same for every part. Nothing has to cross between parts.
Inputs may be any that keep to these rules, and one draw needn't show every extreme that they name: `request_adapter`: among the rows of one device at most 8 name one adapter, and at most 32 name adapters whose slots have the same owner (slot // 4); every device reaches both bounds in every draw. A permutation: adapter a's panels are down_weight[adapter_home_slot[a]] and up_weight[adapter_home_slot[a]].
All inputs are finite; a program needn't handle non-finite values.
Results may differ from a plain program's by a relative error of at most 0.0037.
Values may be sent and summed in bfloat16 or wider, within the bound.
A program may use at most 192 MiB of HBM per device.

v0:
```python
import jax
import jax.numpy as jnp
from jax import lax
from jax.sharding import PartitionSpec as P

MOSTA = 8


def on_device(tokens, value_weight, down_weight, up_weight, request_adapter, adapter_home_slot):
    devices = lax.axis_size("ad")
    model_width = tokens.shape[1]
    resident_count = down_weight.shape[0]
    adapters = adapter_home_slot.shape[0]
    labels = jnp.arange(adapters, dtype=jnp.int32)
    slot_of = jnp.sum(
        jnp.where(request_adapter[:, None] == labels[None, :], adapter_home_slot[None, :], 0),
        axis=1,
    )
    base_output = jnp.dot(
        tokens,
        lax.all_gather(value_weight, "ad", axis=0, tiled=True),
        preferred_element_type=jnp.float32,
    )
    onehot = (slot_of[:, None] == labels[None, :]).astype(jnp.int32)
    position = jnp.sum(onehot * (jnp.cumsum(onehot, axis=0) - 1), axis=1)
    target = slot_of * MOSTA + position
    outgoing = jnp.zeros((adapters * MOSTA, model_width), jnp.bfloat16).at[target].set(tokens)
    outgoing = outgoing.reshape(devices, resident_count, MOSTA, model_width)
    rank_hidden = jnp.einsum(
        "sajd,adr->sajr",
        lax.all_to_all(outgoing, "ad", split_axis=0, concat_axis=0, tiled=True),
        down_weight,
        preferred_element_type=jnp.float32,
    ).astype(jnp.bfloat16)
    adapter_update = (
        0.5
        * jnp.einsum("cbhd,bdn->cbhn", rank_hidden, up_weight, preferred_element_type=jnp.float32)
    ).astype(jnp.bfloat16)
    gathered_back = lax.all_to_all(adapter_update, "ad", split_axis=0, concat_axis=0, tiled=True)
    delta_rows = gathered_back.reshape(adapters * MOSTA, -1)[target]
    return (base_output + delta_rows.astype(jnp.float32)).astype(jnp.bfloat16)


def solution(mesh):
    in_specs = (
        P(("rep", "ad"), None),
        P("ad", None),
        P("ad", None, None),
        P("ad", None, None),
        P(("rep", "ad")),
        P("rep"),
    )
    out_specs = P(("rep", "ad"), None)
    return jax.shard_map(
        on_device, mesh=mesh, in_specs=in_specs, out_specs=out_specs, check_vma=False
    )
```

profile of v0, /device:TPU:8, one launch (start us, length us, event | category | flops | bytes accessed | tf_op | source)
XLA Modules:
  0.0 365.4 jit_solution(2719520194590557017)
XLA Ops:
  6.5 0.0 copy-start
  6.5 0.0 all-gather.2.cloned.1.call-start
  6.5 0.7 all-gather.2.cloned.1.call-update
  7.3 0.8 select_reduce_fusion
  8.1 1.2 reduce-window.6
  9.3 0.2 slice_reduce_fusion
  9.5 0.1 fusion.22
  9.7 18.7 %scatter_custom_fusion = bf16[512,8192]{1,0:T(8,128)(2,1)} fusion(s32[512]{0:T(512)S(1)} %bitcast.47, bf16[512,8192]{1,0:T(8,128)(2,1)} %param.6, bf16[]{:T(256)} %constant.6.clone.1), kind=kCustom, calls=%fused_computation.5 | custom fusion | bytes 8389120 | tf_op jit(solution)/shard_map/scatter | solution.py:27
  28.4 275.7 %all_to_all.10 = bf16[16,4,8,8192]{3,2,1,0:T(8,128)(2,1)} all-to-all(bf16[16,4,8,8192]{3,2,1,0:T(8,128)(2,1)} %bitcast.45), channel_id=1, replica_groups=mesh['rep'=2,'ad'=16] {'ad'}, dimensions={0} | all-to-all | bytes 16777216 | tf_op jit(solution)/shard_map/all_to_all | solution.py:31
  304.1 0.0 copy-done
  304.1 7.2 %fusion.5 = bf16[16,4,8,1024]{3,2,0,1:T(8,128)(2,1)S(1)} fusion(bf16[4,8192,64]{1,2,0:T(8,128)(2,1)} %param.8, bf16[16,4,8,8192]{3,2,1,0:T(8,128)(2,1)} %all_to_all.10, bf16[4,64,1024]{2,1,0:T(8,128)(2,1)S(1)} %copy-done), kind=kOutput, calls=%fused_computation.9 | convolution fusion | flops 605061120 | bytes 14155776 | tf_op jit(solution)/shard_map/cbhd,bdn->cbhn/dot_general | solution.py:37
  311.3 1.1 copy.16
  312.3 4.4 %all-to-all-start.1 = ((bf16[16,4,8,1024]{3,2,1,0:T(8,128)(2,1)}), bf16[16,4,8,1024]{3,2,1,0:T(8,128)(2,1)S(1)}, u32[]{:S(2)}, u32[]{:S(2)}) async-start(bf16[16,4,8,1024]{3,2,1,0:T(8,128)(2,1)} %copy.16), calls=%async_computation.1 | async-start | bytes 2097152 | tf_op jit(solution)/shard_map/all_to_all | solution.py:39
  316.7 24.2 %all-to-all-done.1 = bf16[16,4,8,1024]{3,2,1,0:T(8,128)(2,1)S(1)} async-done(((bf16[16,4,8,1024]{3,2,1,0:T(8,128)(2,1)}), bf16[16,4,8,1024]{3,2,1,0:T(8,128)(2,1)S(1)}, u32[]{:S(2)}, u32[]{:S(2)}) %all-to-all-start.1) | async-done | bytes 1048608 | tf_op jit(solution)/shard_map/all_to_all | solution.py:39
  340.9 2.0 gather_fusion
  343.0 0.0 all-gather.2.cloned.1.call-done
  343.0 15.6 %add_convert_fusion = bf16[512,1024]{1,0:T(8,128)(2,1)} fusion(bf16[512,1024]{1,0:T(8,128)(2,1)S(1)} %gather_fusion, bf16[512,8192]{1,0:T(8,128)(2,1)} %param.6, bf16[8192,1024]{1,0:T(8,128)(2,1)} %all-gather.2.cloned.1.call-done), kind=kOutput, calls=%fused_computation.7 | convolution fusion | flops 8591507456 | bytes 27262976 | tf_op jit(solution)/shard_map/dot_general | solution.py:19
  (6 shorter events, 0.1 us)
Async XLA Ops:
  6.5 297.6 %copy-start = (bf16[4,64,1024]{2,1,0:T(8,128)(2,1)S(1)}, bf16[4,64,1024]{2,1,0:T(8,128)(2,1)}, u32[]{:S(2)}) copy-start(bf16[4,64,1024]{2,1,0:T(8,128)(2,1)} %param.9) | copy-start | bytes 1572868
  6.5 336.4 %all-gather.2.cloned.1.call-start = ((), (), s32[]{:S(2)}) async-start(), calls=%async_computation.2 | async-start | bytes 17825792 | tf_op jit(solution)/shard_map/all_gather | solution.py:21
  312.3 28.6 %all-to-all-start.1 = ((bf16[16,4,8,1024]{3,2,1,0:T(8,128)(2,1)}), bf16[16,4,8,1024]{3,2,1,0:T(8,128)(2,1)S(1)}, u32[]{:S(2)}, u32[]{:S(2)}) async-start(bf16[16,4,8,1024]{3,2,1,0:T(8,128)(2,1)} %copy.16), calls=%async_computation.1 | async-start | bytes 2097152 | tf_op jit(solution)/shard_map/all_to_all | solution.py:39
Sparse Core Ops, SparseCore 0:
  9.5 248.5 all-gather.1
where the time goes:
time: 367 us; the launch traced here: 365 us
  blocking collectives  276 us (75%)
  waiting for transfers between devices  24.9 us (7%)
  matrix products  22.8 us (6%)
  local copies, waits for them, and re-layouts  22 us (6%)
  between operations  13.4 us (4%)
  starting transfers between devices  4.35 us (1%)
    all_to_all x1, blocking collectives, on_device(): lax.all_to_all(outgoing, 'ad', split_axis=0, concat_axis=0, tiled=True)  276 us
    all_to_all x1, waiting for transfers between devices, on_device(): lax.all_to_all(adapter_update, 'ad', split_axis=0, concat_axis=0, tiled=T...  24.2 us
    scatter x1, local copies, waits for them, and re-layouts, on_device(): jnp.zeros((adapters * MOSTA, model_width), jnp.bfloat16).at[target]  18.7 us
    dot_general x1, matrix products, on_device(): jnp.dot(tokens, lax.all_gather(value_weight, 'ad', axis=0, tiled=True), p...  15.6 us
  transfers between devices with their start and end apart: 2, of which 1 were waited for; matrix products, arithmetic and copies ran while one was open for 9% of the time, Pallas kernels for 0%

commit v1 on v0

v1 whole, which is shorter than its diff:
```python
import jax
import jax.numpy as jnp
from jax import lax
from jax.sharding import PartitionSpec as P

MOSTA = 8
PLANE = 8


def solution(mesh):
    reps, devices = mesh.shape["rep"], mesh.shape["ad"]
    inner = PLANE // reps
    layers = devices // inner
    columns = [[z * inner + j for z in range(layers)] for j in range(inner)]
    planes = [
        [r * devices + z * inner + j for r in range(reps) for j in range(inner)]
        for z in range(layers)
    ]

    def on_device(tokens, value_weight, down_weight, up_weight, request_adapter, adapter_home_slot):
        rows, model_width = tokens.shape
        resident = down_weight.shape[0]
        share = resident // reps
        adapters = adapter_home_slot.shape[0]
        rep = lax.axis_index("rep")
        labels = jnp.arange(adapters, dtype=jnp.int32)
        slot_of = jnp.sum(
            jnp.where(request_adapter[:, None] == labels[None, :], adapter_home_slot[None, :], 0),
            axis=1,
        )
        index = jnp.arange(rows, dtype=jnp.int32)
        earlier = (slot_of[:, None] == slot_of[None, :]) & (index[None, :] < index[:, None])
        position = jnp.sum(earlier.astype(jnp.int32), axis=1)
        owner, local = slot_of // resident, slot_of % resident
        layer, lane = owner // inner, owner % inner
        dest = (local // share) * inner + lane
        held = layer * share + local % share
        target = (dest * (layers * share) + held) * MOSTA + position
        places = jnp.arange(adapters * MOSTA, dtype=jnp.int32)
        pick = (places[:, None] == target[None, :]).astype(jnp.bfloat16)
        outgoing = jnp.dot(pick, tokens, preferred_element_type=jnp.float32).astype(jnp.bfloat16)
        outgoing = outgoing.reshape(PLANE, layers * share, MOSTA, model_width)
        incoming = lax.all_to_all(
            outgoing, ("rep", "ad"), split_axis=0, concat_axis=0, tiled=True, axis_index_groups=planes
        )
        down = lax.all_gather(
            lax.dynamic_slice_in_dim(down_weight, rep * share, share, 0),
            "ad", axis=0, tiled=True, axis_index_groups=columns,
        )
        up = lax.all_gather(
            lax.dynamic_slice_in_dim(up_weight, rep * share, share, 0),
            "ad", axis=0, tiled=True, axis_index_groups=columns,
        )
        whole_value = lax.all_gather(value_weight, "ad", axis=0, tiled=True)
        latent = jnp.einsum(
            "sajd,adr->sajr", incoming, down, preferred_element_type=jnp.float32
        ).astype(jnp.bfloat16)
        update = (
            0.5 * jnp.einsum("sajr,arn->sajn", latent, up, preferred_element_type=jnp.float32)
        ).astype(jnp.bfloat16)
        back = lax.all_to_all(
            update, ("rep", "ad"), split_axis=0, concat_axis=0, tiled=True, axis_index_groups=planes
        ).reshape(adapters * MOSTA, -1)
        base = jnp.dot(tokens, whole_value, preferred_element_type=jnp.float32)
        place = (target[:, None] == places[None, :]).astype(jnp.bfloat16)
        delta = jnp.dot(place, back, preferred_element_type=jnp.float32)
        return (base + delta).astype(jnp.bfloat16)

    in_specs = (
        P(("rep", "ad"), None),
        P("ad", None),
        P("ad", None, None),
        P("ad", None, None),
        P(("rep", "ad")),
        P("rep"),
    )
    return jax.shard_map(
        on_device, mesh=mesh, in_specs=in_specs, out_specs=P(("rep", "ad"), None), check_vma=False
    )
```

time: 367 us -> 344 us (0.937)
  blocking collectives: 276 us -> 23.9 us
  waiting for transfers between devices: 24.9 us -> 257 us
  local copies, waits for them, and re-layouts: 22 us -> 4.97 us
  matrix products: 22.8 us -> 35 us
    all_to_all x1, blocking collectives: 276 us -> 23.9 us  [on_device(): lax.all_to_all(update, ('rep', 'ad'), split_axis=0, concat_axis=0, tiled=...]
    all_gather x1 -> x3, waiting for transfers between devices: 0.02 us -> 173 us  [the longest x1 98.8 us: on_device(): whole_value = lax.all_gather(value_weight, 'ad', axis=0, tiled=True)]
    all_to_all x1, waiting for transfers between devices: 24.2 us -> 83.5 us  [on_device(): lax.all_to_all(outgoing, ('rep', 'ad'), split_axis=0, concat_axis=0, tile...]
    scatter x1 -> x0, local copies, waits for them, and re-layouts: 18.7 us -> none  [on_device(): jnp.zeros((adapters * MOSTA, model_width), jnp.bfloat16).at[target]]
    dot_general x2 -> x4, matrix products: 22.8 us -> 35 us  [the longest x1 15.6 us: on_device(): base = jnp.dot(tokens, whole_value, preferred_element_type=jnp.float32)]
    dynamic_slice x0 -> x2, local copies, waits for them, and re-layouts: none -> 3.85 us  [the longest x1 3.13 us: on_device(): lax.dynamic_slice_in_dim(down_weight, rep * share, share, 0)]
  transfers between devices with their start and end apart: 2 -> 4, of which waited for: 1 -> 4; matrix products, arithmetic and copies ran while one was open for 9% -> 7% of each run, Pallas kernels for 0% -> 0%
where the time goes in v1:
time: 344 us; the launch traced here: 340 us
  waiting for transfers between devices  257 us (75%)
  matrix products  35 us (10%)
  blocking collectives  23.9 us (7%)
  between operations  13.1 us (4%)
  starting transfers between devices  5.12 us (1%)
  local copies, waits for them, and re-layouts  4.97 us (1%)
    all_gather x1, waiting for transfers between devices, on_device(): whole_value = lax.all_gather(value_weight, 'ad', axis=0, tiled=True)  98.8 us
    all_to_all x1, waiting for transfers between devices, on_device(): lax.all_to_all(outgoing, ('rep', 'ad'), split_axis=0, concat_axis=0, tile...  83.5 us
    all_gather x1, waiting for transfers between devices, on_device(): lax.all_gather(lax.dynamic_slice_in_dim(down_weight, rep * share, share,...  64.2 us
    all_to_all x1, blocking collectives, on_device(): lax.all_to_all(update, ('rep', 'ad'), split_axis=0, concat_axis=0, tiled=...  23.9 us
    dot_general x1, matrix products, on_device(): base = jnp.dot(tokens, whole_value, preferred_element_type=jnp.float32)  15.6 us
    dot_general x1, matrix products, on_device(): jnp.dot(pick, tokens, preferred_element_type=jnp.float32)  10.1 us
    all_gather x1, waiting for transfers between devices, on_device(): lax.all_gather(lax.dynamic_slice_in_dim(up_weight, rep * share, share, 0)...  9.57 us
    dot_general x1, matrix products, on_device(): jnp.einsum('sajr,arn->sajn', latent, up, preferred_element_type=jnp.float32)  8.65 us
  transfers between devices with their start and end apart: 4, of which 4 were waited for; matrix products, arithmetic and copies ran while one was open for 7% of the time, Pallas kernels for 0%

profile of v1, /device:TPU:8, one launch (start us, length us, event | category | flops | bytes accessed | tf_op | source)
XLA Modules:
  0.0 340.1 jit_solution(15042444832742469361)
XLA Ops:
  6.5 0.0 copy-start
  6.5 0.0 all-gather.6.cloned.1.call-start
  6.5 1.0 copy-done
  7.6 0.7 constant_dynamic-slice_fusion
  8.3 0.0 all-gather.6.cloned.1.call-update
  8.3 0.0 all-gather.8.cloned.1.call-start
  8.4 3.1 constant_dynamic-slice_fusion.1
  11.5 0.0 all-gather.8.cloned.1.call-update
  11.5 0.0 all-gather.4.cloned.1.call-start
  11.6 0.7 all-gather.4.cloned.1.call-update
  12.3 0.8 select_reduce_fusion
  13.1 0.3 convert_reduce_fusion
  13.3 10.1 %convolution_convert_fusion = bf16[512,8192]{1,0:T(8,128)(2,1)} fusion(bf16[512,8192]{1,0:T(8,128)(2,1)} %param.6, s32[512]{0:T(512)S(1)} %fusion.28), kind=kOutput, calls=%fused_computation | convolution fusion | flops 4299423744 | bytes 16779264 | tf_op jit(solution)/shard_map/dot_general | solution.py:41
  23.4 5.0 %all-to-all-start = ((bf16[8,8,8,8192]{3,2,1,0:T(8,128)(2,1)}), bf16[8,8,8,8192]{3,2,1,0:T(8,128)(2,1)}, u32[]{:S(2)}, u32[]{:S(2)}) async-start(bf16[8,8,8,8192]{3,2,1,0:T(8,128)(2,1)} %bitcast.28), calls=%async_computation | async-start | bytes 16777216 | tf_op jit(solution)/shard_map/all_to_all | solution.py:43
  28.5 9.6 %all-gather.6.cloned.1.call-done = bf16[8,64,1024]{2,1,0:T(8,128)(2,1)} async-done(((bf16[2,64,1024]{2,1,0:T(8,128)(2,1)}), bf16[8,64,1024]{2,1,0:T(8,128)(2,1)}) %all-gather.6.cloned.1.call-update) | async-done | bytes 1048592 | tf_op jit(solution)/shard_map/all_gather | solution.py:50
  38.0 83.5 %all-to-all-done = bf16[8,8,8,8192]{3,2,1,0:T(8,128)(2,1)} async-done(((bf16[8,8,8,8192]{3,2,1,0:T(8,128)(2,1)}), bf16[8,8,8,8192]{3,2,1,0:T(8,128)(2,1)}, u32[]{:S(2)}, u32[]{:S(2)}) %all-to-all-start) | async-done | bytes 8388640 | tf_op jit(solution)/shard_map/all_to_all | solution.py:43
  121.6 64.2 %all-gather.8.cloned.1.call-done = bf16[8,8192,64]{1,2,0:T(8,128)(2,1)} async-done(((bf16[2,8192,64]{1,2,0:T(8,128)(2,1)}), bf16[8,8192,64]{1,2,0:T(8,128)(2,1)}) %all-gather.8.cloned.1.call-update) | async-done | bytes 8388624 | tf_op jit(solution)/shard_map/all_gather | solution.py:46
  185.8 8.7 %fusion.3 = bf16[8,8,8,1024]{3,2,0,1:T(8,128)(2,1)S(1)} fusion(bf16[8,8,8,8192]{3,2,1,0:T(8,128)(2,1)} %all-to-all-done, bf16[8,8192,64]{1,2,0:T(8,128)(2,1)} %all-gather.8.cloned.1.call-done, bf16[8,64,1024]{2,1,0:T(8,128)(2,1)} %all-gather.6.cloned.1.call-done), kind=kOutput, calls=%fused_computation.6 | convolution fusion | flops 605061120 | bytes 18874368 | tf_op jit(solution)/shard_map/sajr,arn->sajn/dot_general | solution.py:59
  194.5 0.1 copy.13
  194.5 23.9 %all_to_all.10 = bf16[8,8,8,1024]{3,2,1,0:T(8,128)(2,1)S(1)} all-to-all(bf16[8,8,8,1024]{3,2,1,0:T(8,128)(2,1)S(1)} %copy.13), channel_id=1, replica_groups={{0,1,2,3,16,17,18,19},{4,5,6,7,20,21,22,23},{8,9,10,11,24,25,26,27},{12..., dimensions={0} | all-to-all | bytes 2097152 | tf_op jit(solution)/shard_map/all_to_all | solution.py:61
  218.5 0.8 fusion.20
  219.2 98.8 %all-gather.4.cloned.1.call-done = bf16[8192,1024]{1,0:T(8,128)(2,1)} async-done(((bf16[512,1024]{1,0:T(8,128)(2,1)}), bf16[8192,1024]{1,0:T(8,128)(2,1)}) %all-gather.4.cloned.1.call-update) | async-done | bytes 16777232 | tf_op jit(solution)/shard_map/all_gather | solution.py:54
  318.1 15.6 %add_convert_fusion = bf16[512,1024]{1,0:T(8,128)(2,1)} fusion(f32[512,1024]{1,0:T(8,128)S(1)} %fusion.20, bf16[512,8192]{1,0:T(8,128)(2,1)} %param.6, bf16[8192,1024]{1,0:T(8,128)(2,1)} %all-gather.4.cloned.1.call-done), kind=kOutput, calls=%fused_computation.4 | convolution fusion | flops 8590983168 | bytes 28311552 | tf_op jit(solution)/shard_map/dot_general | solution.py:64
  (1 shorter events, 0.0 us)
Async XLA Ops:
  6.5 1.0 copy-start
  6.5 31.5 %all-gather.6.cloned.1.call-start = ((), (), s32[]{:S(2)}) async-start(), calls=%async_computation.3 | async-start | bytes 1310720 | tf_op jit(solution)/shard_map/all_gather | solution.py:50
  8.3 177.5 %all-gather.8.cloned.1.call-start = ((), (), s32[]{:S(2)}) async-start(), calls=%async_computation.4 | async-start | bytes 10485760 | tf_op jit(solution)/shard_map/all_gather | solution.py:46
  11.5 306.5 %all-gather.4.cloned.1.call-start = ((), (), s32[]{:S(2)}) async-start(), calls=%async_computation.2 | async-start | bytes 17825792 | tf_op jit(solution)/shard_map/all_gather | solution.py:54
  23.4 98.2 %all-to-all-start = ((bf16[8,8,8,8192]{3,2,1,0:T(8,128)(2,1)}), bf16[8,8,8,8192]{3,2,1,0:T(8,128)(2,1)}, u32[]{:S(2)}, u32[]{:S(2)}) async-start(bf16[8,8,8,8192]{3,2,1,0:T(8,128)(2,1)} %bitcast.28), calls=%async_computation | async-start | bytes 16777216 | tf_op jit(solution)/shard_map/all_to_all | solution.py:43
Sparse Core Ops, SparseCore 0:
  8.9 29.0 all-gather.5
  39.6 146.1 all-gather.7
  188.0 130.0 all-gather.3

commit v2 on v1

v2 whole, which is shorter than its diff:
```python
import jax
import jax.numpy as jnp
from jax import lax
from jax.sharding import PartitionSpec as P

MOSTA = 8
PLANE = 8
F32 = jnp.float32
BF16 = jnp.bfloat16


def solution(mesh):
    reps, devices = mesh.shape["rep"], mesh.shape["ad"]
    inner = PLANE // reps
    layers = devices // inner
    relayed = layers == 4
    columns = [[z * inner + j for z in range(layers)] for j in range(inner)]
    planes = [
        [r * devices + z * inner + j for r in range(reps) for j in range(inner)]
        for z in range(layers)
    ]
    same_core = [list(range(c, devices, 2)) for c in range(2)]
    core_swap = [(i, i ^ 1) for i in range(devices)]

    def hop(array, *pairs):
        moves = [(a * inner + j, b * inner + j) for a, b in pairs for j in range(inner)]
        return lax.ppermute(array, "ad", moves)

    def exchange(array):
        return lax.all_to_all(
            array, ("rep", "ad"), split_axis=0, concat_axis=0, tiled=True, axis_index_groups=planes
        )

    def adapt(rows, panel, model_width):
        latent = jnp.einsum(
            "sajd,ard->sajr", rows, panel[:, :, :model_width], preferred_element_type=F32
        ).astype(BF16)
        return (
            0.5 * jnp.einsum("sajr,arn->sajn", latent, panel[:, :, model_width:], preferred_element_type=F32)
        ).astype(BF16)

    def after(array, earlier):
        return lax.optimization_barrier((array, earlier))[0]

    def whole_value(value_weight, earlier):
        mine = lax.all_gather(value_weight, "ad", axis=0, tiled=False, axis_index_groups=same_core)
        mine = after(mine, earlier)
        other = lax.ppermute(mine, "ad", core_swap)
        first = lax.axis_index("ad") % 2 == 0
        both = jnp.stack([jnp.where(first, mine, other), jnp.where(first, other, mine)], axis=1)
        return both.reshape(-1, value_weight.shape[1])

    def on_device(tokens, value_weight, down_weight, up_weight, request_adapter, adapter_home_slot):
        rows, model_width = tokens.shape
        resident = down_weight.shape[0]
        share = resident // reps
        adapters = adapter_home_slot.shape[0]
        rep = lax.axis_index("rep")
        here = lax.axis_index("ad") // inner
        own = jnp.concatenate(
            [
                lax.dynamic_slice_in_dim(down_weight, rep * share, share, 0).transpose(0, 2, 1),
                lax.dynamic_slice_in_dim(up_weight, rep * share, share, 0),
            ],
            axis=2,
        )
        labels = jnp.arange(adapters, dtype=jnp.int32)
        slot_of = jnp.sum(
            jnp.where(request_adapter[:, None] == labels[None, :], adapter_home_slot[None, :], 0),
            axis=1,
        )
        index = jnp.arange(rows, dtype=jnp.int32)
        earlier = (slot_of[:, None] == slot_of[None, :]) & (index[None, :] < index[:, None])
        position = jnp.sum(earlier.astype(jnp.int32), axis=1)
        owner, local = slot_of // resident, slot_of % resident
        layer, lane = owner // inner, owner % inner
        dest = (local // share) * inner + lane
        if relayed:
            low = here < 2
            middle = jnp.where(low, 2, 1)
            block = jnp.where(
                layer == here, 0, jnp.where(layer == here ^ 1, 1, jnp.where(layer == middle, 2, 3))
            )
        else:
            block = layer
        within = (local % share) * MOSTA + position
        span = share * MOSTA

        def places(start, count):
            at = jnp.arange(PLANE * count * span, dtype=jnp.int32)
            far = at // span
            return (far // count) * layers * span + (start + far % count) * span + at % span

        target = (dest * layers + block) * span + within

        def outgoing(start, count):
            pick = (places(start, count)[:, None] == target[None, :]).astype(BF16)
            sent = jnp.dot(pick, tokens, preferred_element_type=F32).astype(BF16)
            return sent.reshape(PLANE, count * share, MOSTA, model_width)

        def delta(update, start, count):
            pick = (target[:, None] == places(start, count)[None, :]).astype(BF16)
            return jnp.dot(pick, update.reshape(PLANE * count * span, -1), preferred_element_type=F32)

        def joined(parts):
            return jnp.concatenate(parts, axis=1)

        if relayed:
            edge = (here == 0) | (here == 3)
            far_rows = exchange(outgoing(3, 1))
            near_sent = outgoing(0, 3)
            near_rows = exchange(near_sent)
            pair = after(hop(own, (0, 1), (1, 0), (2, 3), (3, 2)), near_sent)
            mid = after(hop(own, (1, 2), (2, 1)), near_sent)
            crossed = hop(pair, (1, 2), (2, 1))
            outer = hop(mid, (1, 0), (2, 3))
            extra_rows = hop(far_rows, (0, 1), (3, 2))
            base = jnp.dot(tokens, whole_value(value_weight, near_sent), preferred_element_type=F32)
            extra = hop(adapt(extra_rows, crossed, model_width), (1, 0), (2, 3))
            far = jnp.where(edge, extra, adapt(far_rows, crossed, model_width))
            panels = jnp.concatenate([own, pair, jnp.where(edge, outer, mid)], axis=0)
            near = adapt(near_rows, panels, model_width)
            back = exchange(joined([near, far]))
        else:
            sent = outgoing(0, layers)
            incoming = exchange(sent)
            panels = lax.all_gather(own, "ad", axis=0, tiled=True, axis_index_groups=columns)
            base = jnp.dot(tokens, whole_value(value_weight, sent), preferred_element_type=F32)
            back = exchange(adapt(incoming, panels, model_width))
        return (base + delta(back, 0, layers)).astype(BF16)

    in_specs = (
        P(("rep", "ad"), None),
        P("ad", None),
        P("ad", None, None),
        P("ad", None, None),
        P(("rep", "ad")),
        P("rep"),
    )
    return jax.shard_map(
        on_device, mesh=mesh, in_specs=in_specs, out_specs=P(("rep", "ad"), None), check_vma=False
    )
```

time: 344 us -> 313 us (0.910)
  waiting for transfers between devices: 257 us -> 198 us
  blocking collectives: 23.9 us -> 0 us
  starting transfers between devices: 5.12 us -> 28.8 us
  other arithmetic: 1.07 us -> 18.7 us
  matrix products: 35 us -> 43.4 us
    all_to_all x1 -> x3, waiting for transfers between devices: 83.5 us -> 16.1 us  [exchange(): lax.all_to_all(array, ('rep', 'ad'), split_axis=0, concat_axis=0, tiled=T...]
    ppermute x0 -> x7, waiting for transfers between devices: none -> 45.9 us  [the longest x6 45.9 us: hop(): return lax.ppermute(array, 'ad', moves)]
    all_gather x3 -> x1, waiting for transfers between devices: 173 us -> 135 us  [whole_value(): lax.all_gather(value_weight, 'ad', axis=0, tiled=False, axis_index_groups...]
    all_to_all x1 -> x0, blocking collectives: 23.9 us -> none  [on_device(): lax.all_to_all(update, ('rep', 'ad'), split_axis=0, concat_axis=0, tiled=...]
    ppermute x0 -> x7, starting transfers between devices: none -> 16 us  [the longest x6 15.9 us: hop(): return lax.ppermute(array, 'ad', moves)]
    another operation x0 -> x2, other arithmetic: none -> 13.2 us  [whole_value(): jnp.stack([jnp.where(first, mine, other), jnp.where(first, other, mine)],...]
    dot_general x4 -> x7, matrix products: 35 us -> 43.4 us  [the longest x2 15 us: outgoing(): sent = jnp.dot(pick, tokens, preferred_element_type=F32).astype(BF16)]
    all_to_all x1 -> x3, starting transfers between devices: 5.04 us -> 12.9 us  [exchange(): lax.all_to_all(array, ('rep', 'ad'), split_axis=0, concat_axis=0, tiled=T...]
  transfers between devices with their start and end apart: 4 -> 11, of which waited for: 4 -> 5; matrix products, arithmetic and copies ran while one was open for 7% -> 13% of each run, Pallas kernels for 0% -> 0%
where the time goes in v2:
time: 313 us; the launch traced here: 310 us
  waiting for transfers between devices  198 us (63%)
  matrix products  43.4 us (14%)
  starting transfers between devices  28.8 us (9%)
  other arithmetic  18.7 us (6%)
  between operations  13.6 us (4%)
  local copies, waits for them, and re-layouts  7.55 us (2%)
    all_gather x1, waiting for transfers between devices, whole_value(): lax.all_gather(value_weight, 'ad', axis=0, tiled=False, axis_index_groups...  135 us
    ppermute x6, waiting for transfers between devices, hop(): return lax.ppermute(array, 'ad', moves)  45.9 us
    all_to_all x3, waiting for transfers between devices, exchange(): lax.all_to_all(array, ('rep', 'ad'), split_axis=0, concat_axis=0, tiled=T...  16.1 us
    ppermute x6, starting transfers between devices, hop(): return lax.ppermute(array, 'ad', moves)  15.9 us
    dot_general x2, matrix products, outgoing(): sent = jnp.dot(pick, tokens, preferred_element_type=F32).astype(BF16)  15 us
    dot_general x1, matrix products, on_device(): jnp.dot(tokens, whole_value(value_weight, near_sent), preferred_element_t...  14.9 us
    another operation x2, other arithmetic, whole_value(): jnp.stack([jnp.where(first, mine, other), jnp.where(first, other, mine)],...  13.2 us
    all_to_all x3, starting transfers between devices, exchange(): lax.all_to_all(array, ('rep', 'ad'), split_axis=0, concat_axis=0, tiled=T...  12.9 us
  transfers between devices with their start and end apart: 11, of which 5 were waited for; matrix products, arithmetic and copies ran while one was open for 13% of the time, Pallas kernels for 0%

profile of v2, /device:TPU:8, one launch (start us, length us, event | category | flops | bytes accessed | tf_op | source)
XLA Modules:
  0.0 310.0 jit_solution(1108499973583524401)
XLA Ops:
  6.5 0.0 copy-start
  6.5 0.0 all-gather.3.cloned.1.call-start
  6.5 0.7 all-gather.3.cloned.1.call-update
  7.3 0.3 copy-done
  7.6 1.8 dynamic-slice_bitcast_fusion
  9.4 0.0 copy-start.2
  9.4 0.0 copy-start.3
  9.4 1.6 pad_maximum_fusion.6
  11.0 3.5 %collective-permute-start.2 = (bf16[2,64,9216]{2,1,0:T(8,128)(2,1)}, bf16[2,64,9216]{2,1,0:T(8,128)(2,1)}, u32[]{:S(2)}, u32[]{:S(2)}) collective-permute-start(bf16[2,64,9216]{2,1,0:T(8,128)(2,1)} %pad_maximum_fusion.6), channel_id=1, source_target_pairs={{4,8},{5,9},{6,10},{7,11},{8,4},{9,5},{10,6},{11,7},{20,24},{21,25... | collective-permute-start | bytes 7077896 | tf_op jit(solution)/shard_map/ppermute | solution.py:27
  14.5 0.1 collective-permute-start.1
  14.6 0.0 copy-done.2
  14.6 0.0 copy-done.3
  14.6 0.1 select_reduce_fusion
  14.7 0.3 convert_reduce_fusion
  15.0 6.1 %convolution_convert_fusion.1 = bf16[128,8192]{1,0:T(8,128)(2,1)} fusion(bf16[512,8192]{1,0:T(8,128)(2,1)} %param.6, s32[512]{0:T(512)S(1)} %fusion.64, s32[128]{0:T(128)S(1)} %fusion.94), kind=kOutput, calls=%fused_computation.2 | convolution fusion | flops 1074855936 | bytes 10488320 | tf_op jit(solution)/shard_map/dot_general | solution.py:98
  21.1 4.3 %all-to-all-start.1 = ((bf16[8,2,8,8192]{3,2,1,0:T(8,128)(2,1)}), bf16[8,2,8,8192]{3,2,1,0:T(8,128)(2,1)}, u32[]{:S(2)}, u32[]{:S(2)}) async-start(bf16[8,2,8,8192]{3,2,1,0:T(8,128)(2,1)} %bitcast.84), calls=%async_computation.1 | async-start | bytes 4194304 | tf_op jit(solution)/shard_map/all_to_all | solution.py:30
  25.5 8.8 %convolution_convert_fusion = bf16[384,8192]{1,0:T(8,128)(2,1)} fusion(bf16[512,8192]{1,0:T(8,128)(2,1)} %param.6, s32[512]{0:T(512)S(1)} %fusion.64, s32[384]{0:T(512)S(1)} %fusion.58), kind=kOutput, calls=%fused_computation.1 | convolution fusion | flops 3224567808 | bytes 14683648 | tf_op jit(solution)/shard_map/dot_general | solution.py:98
  34.3 135.2 %all-gather.3.cloned.1.call-done = bf16[4096,1024]{1,0:T(8,128)(2,1)} async-done(((bf16[512,1024]{1,0:T(8,128)(2,1)}), bf16[4096,1024]{1,0:T(8,128)(2,1)}) %all-gather.3.cloned.1.call-update) | async-done | bytes 8388624 | tf_op jit(solution)/shard_map/all_gather | solution.py:46
  169.6 0.1 collective-permute-start
  169.6 0.0 collective-permute-done.1
  169.6 2.3 collective-permute-start.4
  172.0 0.0 all-to-all-done.1
  172.0 4.8 %all-to-all-start = ((bf16[8,6,8,8192]{3,2,1,0:T(8,128)(2,1)}), bf16[8,6,8,8192]{3,2,1,0:T(8,128)(2,1)}, u32[]{:S(2)}, u32[]{:S(2)}) async-start(bf16[8,6,8,8192]{3,2,1,0:T(8,128)(2,1)} %bitcast.85), calls=%async_computation | async-start | bytes 12582912 | tf_op jit(solution)/shard_map/all_to_all | solution.py:30
  176.8 3.0 copy.28
  179.8 1.3 collective-permute-start.5
  181.1 0.0 collective-permute-done.2
  181.1 7.3 %collective-permute-start.3 = (bf16[2,64,9216]{2,1,0:T(8,128)(2,1)}, bf16[2,64,9216]{2,1,0:T(8,128)(2,1)}, u32[]{:S(2)}, u32[]{:S(2)}) collective-permute-start(bf16[2,64,9216]{2,1,0:T(8,128)(2,1)} %collective-permute-done.2), channel_id=1, source_target_pairs={{4,0},{5,1},{6,2},{7,3},{8,12},{9,13},{10,14},{11,15},{20,16},{21,... | collective-permute-start | bytes 7077896 | tf_op jit(solution)/shard_map/ppermute | solution.py:27
  188.4 41.5 %collective-permute-done.5 = bf16[8,2,8,8192]{3,2,0,1:T(8,128)(2,1)} collective-permute-done((bf16[8,2,8,8192]{3,2,0,1:T(8,128)(2,1)}, bf16[8,2,8,8192]{3,2,0,1:T(8,128)(2,1)}, u32[]{:S(2)}, u32[]{:S(2)}) %collective-permute-start.5) | collective-permute-done | bytes 2097184 | tf_op jit(solution)/shard_map/ppermute | solution.py:27
  229.9 0.0 collective-permute-done.4
  229.9 3.2 %fusion.12 = bf16[8,2,8,1024]{3,2,0,1:T(8,128)(2,1)S(1)} fusion(bf16[8,2,8,8192]{3,2,0,1:T(8,128)(2,1)} %collective-permute-done.5, bf16[2,64,9216]{2,1,0:T(8,128)(2,1)} %collective-permute-done.4), kind=kOutput, calls=%fused_computation.27 | convolution fusion | flops 151265280 | bytes 4718592 | tf_op jit(solution)/shard_map/sajr,arn->sajn/dot_general | solution.py:39
  233.1 1.5 collective-permute-start.6
  234.6 4.4 %collective-permute-done.3 = bf16[2,64,9216]{2,1,0:T(8,128)(2,1)} collective-permute-done((bf16[2,64,9216]{2,1,0:T(8,128)(2,1)}, bf16[2,64,9216]{2,1,0:T(8,128)(2,1)}, u32[]{:S(2)}, u32[]{:S(2)}) %collective-permute-start.3) | collective-permute-done | bytes 2359328 | tf_op jit(solution)/shard_map/ppermute | solution.py:27
  238.9 3.3 %broadcast_select_fusion = bf16[2,64,9216]{2,1,0:T(8,128)(2,1)} fusion(bf16[2,64,9216]{2,1,0:T(8,128)(2,1)} %collective-permute-done.3, bf16[2,64,9216]{2,1,0:T(8,128)(2,1)} %collective-permute-done.2, pred[]{:T(512)S(6)} %or.3), kind=kLoop, calls=%fused_computation.13 | loop fusion | flops 1179648 | bytes 7077889 | tf_op jit(solution)/shard_map/jit(_where)/select_n | solution.py:121
  242.3 3.2 %fusion.11 = bf16[8,2,8,1024]{3,2,0,1:T(8,128)(2,1)S(1)} fusion(bf16[2,64,9216]{2,1,0:T(8,128)(2,1)} %collective-permute-done.4, bf16[8,2,8,8192]{3,2,1,0:T(8,128)(2,1)} %all-to-all-done.1), kind=kOutput, calls=%fused_computation.26 | convolution fusion | flops 151265280 | bytes 4718592 | tf_op jit(solution)/shard_map/sajr,arn->sajn/dot_general | solution.py:39
  245.5 0.0 collective-permute-done.6
  245.5 1.9 all-to-all-done
  247.4 6.2 %fusion.8 = bf16[8,6,8,1024]{3,2,0,1:T(8,128)(2,1)S(1)} fusion(bf16[8,6,8,8192]{3,2,1,0:T(8,128)(2,1)} %all-to-all-done, bf16[2,64,9216]{2,1,0:T(8,128)(2,1)} %broadcast_select_fusion, bf16[2,64,9216]{2,1,0:T(8,128)(2,1)} %collective-permute-done.1, bf16[2,64,1024]{2,1,0:T(8,128)(2,1)S(1)} %constant_dynamic-slice_fusion, ...), kind=kOutput, calls=%fused_computation.21 | convolution fusion | flops 482107392 | bytes 14155776 | tf_op jit(solution)/shard_map/sajr,arn->sajn/dot_general | solution.py:39
  253.6 0.1 pad_maximum_fusion.7
  253.7 1.1 copy.30
  254.8 3.7 %all-to-all-start.2 = ((bf16[8,8,8,1024]{3,2,1,0:T(8,128)(2,1)}), bf16[8,8,8,1024]{3,2,1,0:T(8,128)(2,1)S(1)}, u32[]{:S(2)}, u32[]{:S(2)}) async-start(bf16[8,8,8,1024]{3,2,1,0:T(8,128)(2,1)} %copy.30), calls=%async_computation.2 | async-start | bytes 2097152 | tf_op jit(solution)/shard_map/all_to_all | solution.py:30
  258.6 14.2 %all-to-all-done.2 = bf16[8,8,8,1024]{3,2,1,0:T(8,128)(2,1)S(1)} async-done(((bf16[8,8,8,1024]{3,2,1,0:T(8,128)(2,1)}), bf16[8,8,8,1024]{3,2,1,0:T(8,128)(2,1)S(1)}, u32[]{:S(2)}, u32[]{:S(2)}) %all-to-all-start.2) | async-done | bytes 1048608 | tf_op jit(solution)/shard_map/all_to_all | solution.py:30
  272.7 0.9 fusion.32
  273.6 0.0 collective-permute-done
  273.6 6.5 %select_bitcast_fusion.1 = (bf16[8,1,512,1024]{3,2,1,0:T(8,128)(2,1)S(1)}, bf16[8,1,512,1024]{3,2,1,0:T(8,128)(2,1)S(1)}) fusion(bf16[8,512,1024]{2,1,0:T(8,128)(2,1)} %bitcast.83, bf16[8,512,1024]{2,1,0:T(8,128)(2,1)} %collective-permute-done, pred[]{:T(512)S(6)} %eq.130), kind=kLoop, calls=%fused_computation.4 | loop fusion | flops 8388608 | bytes 33554432 | tf_op jit(solution)/shard_map/stack | solution.py:50
  280.1 6.8 %pad_maximum_fusion = bf16[8,2,512,1024]{3,2,1,0:T(8,128)(2,1)} fusion(bf16[8,1,512,1024]{3,2,1,0:T(8,128)(2,1)S(1)} %get-tuple-element.12, bf16[8,1,512,1024]{3,2,1,0:T(8,128)(2,1)S(1)} %get-tuple-element.11), kind=kLoop, calls=%fused_computation | loop fusion | flops 8388608 | bytes 33554432 | tf_op jit(solution)/shard_map/stack | solution.py:50
  286.9 0.0 copy-start.1
  286.9 14.9 %fusion.5 = bf16[512,1024]{0,1:T(8,128)(2,1)S(1)} fusion(f32[512,1024]{0,1:T(8,128)S(1)} %fusion.32, bf16[8192,1024]{1,0:T(8,128)(2,1)} %bitcast.81, bf16[512,8192]{1,0:T(8,128)(2,1)} %param.6), kind=kOutput, calls=%fused_computation.16 | convolution fusion | flops 8590983168 | bytes 28311552 | tf_op jit(solution)/shard_map/dot_general | solution.py:118
  301.9 1.3 copy.32
  303.2 0.0 copy-done.1
  (6 shorter events, 0.1 us)
Async XLA Ops:
  6.5 1.0 copy-start
  6.5 163.0 %all-gather.3.cloned.1.call-start = ((), (), s32[]{:S(2)}) async-start(), calls=%async_computation.3 | async-start | bytes 9437184 | tf_op jit(solution)/shard_map/all_gather | solution.py:46
  9.4 5.2 %copy-start.2 = (s32[512]{0:T(512)S(1)}, s32[512]{0:T(512)}, u32[]{:S(2)}) copy-start(s32[512]{0:T(512)} %param.10) | copy-start | bytes 6148
  9.4 5.2 %copy-start.3 = (s32[64]{0:T(128)S(1)}, s32[64]{0:T(128)}, u32[]{:S(2)}) copy-start(s32[64]{0:T(128)} %param.11) | copy-start | bytes 772
  11.0 170.1 %collective-permute-start.2 = (bf16[2,64,9216]{2,1,0:T(8,128)(2,1)}, bf16[2,64,9216]{2,1,0:T(8,128)(2,1)}, u32[]{:S(2)}, u32[]{:S(2)}) collective-permute-start(bf16[2,64,9216]{2,1,0:T(8,128)(2,1)} %pad_maximum_fusion.6), channel_id=1, source_target_pairs={{4,8},{5,9},{6,10},{7,11},{8,4},{9,5},{10,6},{11,7},{20,24},{21,25... | collective-permute-start | bytes 7077896 | tf_op jit(solution)/shard_map/ppermute | solution.py:27
  14.5 155.1 %collective-permute-start.1 = (bf16[2,64,9216]{2,1,0:T(8,128)(2,1)}, bf16[2,64,9216]{2,1,0:T(8,128)(2,1)}, u32[]{:S(2)}, u32[]{:S(2)}) collective-permute-start(bf16[2,64,9216]{2,1,0:T(8,128)(2,1)} %pad_maximum_fusion.6), channel_id=1, source_target_pairs={{0,4},{1,5},{2,6},{3,7},{4,0},{5,1},{6,2},{7,3},{8,12},{9,13},{10,... | collective-permute-start | bytes 7077896 | tf_op jit(solution)/shard_map/ppermute | solution.py:27
  21.1 150.8 %all-to-all-start.1 = ((bf16[8,2,8,8192]{3,2,1,0:T(8,128)(2,1)}), bf16[8,2,8,8192]{3,2,1,0:T(8,128)(2,1)}, u32[]{:S(2)}, u32[]{:S(2)}) async-start(bf16[8,2,8,8192]{3,2,1,0:T(8,128)(2,1)} %bitcast.84), calls=%async_computation.1 | async-start | bytes 4194304 | tf_op jit(solution)/shard_map/all_to_all | solution.py:30
  169.6 104.1 %collective-permute-start = (bf16[8,512,1024]{2,1,0:T(8,128)(2,1)}, bf16[8,512,1024]{2,1,0:T(8,128)(2,1)}, u32[]{:S(2)}, u32[]{:S(2)}) collective-permute-start(bf16[8,512,1024]{2,1,0:T(8,128)(2,1)} %bitcast.82), channel_id=1, source_target_pairs={{0,1},{1,0},{2,3},{3,2},{4,5},{5,4},{6,7},{7,6},{8,9},{9,8},{10,11... | collective-permute-start | bytes 25165832 | tf_op jit(solution)/shard_map/ppermute | solution.py:48
  169.6 60.3 %collective-permute-start.4 = (bf16[2,64,9216]{2,1,0:T(8,128)(2,1)}, bf16[2,64,9216]{2,1,0:T(8,128)(2,1)}, u32[]{:S(2)}, u32[]{:S(2)}) collective-permute-start(bf16[2,64,9216]{2,1,0:T(8,128)(2,1)} %collective-permute-done.1), channel_id=1, source_target_pairs={{4,8},{5,9},{6,10},{7,11},{8,4},{9,5},{10,6},{11,7},{20,24},{21,25... | collective-permute-start | bytes 7077896 | tf_op jit(solution)/shard_map/ppermute | solution.py:27
  172.0 75.4 %all-to-all-start = ((bf16[8,6,8,8192]{3,2,1,0:T(8,128)(2,1)}), bf16[8,6,8,8192]{3,2,1,0:T(8,128)(2,1)}, u32[]{:S(2)}, u32[]{:S(2)}) async-start(bf16[8,6,8,8192]{3,2,1,0:T(8,128)(2,1)} %bitcast.85), calls=%async_computation | async-start | bytes 12582912 | tf_op jit(solution)/shard_map/all_to_all | solution.py:30
  179.8 50.1 %collective-permute-start.5 = (bf16[8,2,8,8192]{3,2,0,1:T(8,128)(2,1)}, bf16[8,2,8,8192]{3,2,0,1:T(8,128)(2,1)}, u32[]{:S(2)}, u32[]{:S(2)}) collective-permute-start(bf16[8,2,8,8192]{3,2,0,1:T(8,128)(2,1)} %copy.28), channel_id=1, source_target_pairs={{0,4},{1,5},{2,6},{3,7},{12,8},{13,9},{14,10},{15,11},{16,20},{17,... | collective-permute-start | bytes 6291464 | tf_op jit(solution)/shard_map/ppermute | solution.py:27
  181.1 57.8 %collective-permute-start.3 = (bf16[2,64,9216]{2,1,0:T(8,128)(2,1)}, bf16[2,64,9216]{2,1,0:T(8,128)(2,1)}, u32[]{:S(2)}, u32[]{:S(2)}) collective-permute-start(bf16[2,64,9216]{2,1,0:T(8,128)(2,1)} %collective-permute-done.2), channel_id=1, source_target_pairs={{4,0},{5,1},{6,2},{7,3},{8,12},{9,13},{10,14},{11,15},{20,16},{21,... | collective-permute-start | bytes 7077896 | tf_op jit(solution)/shard_map/ppermute | solution.py:27
  233.1 12.4 %collective-permute-start.6 = (bf16[8,2,8,1024]{3,2,0,1:T(8,128)(2,1)S(1)}, bf16[8,2,8,1024]{3,2,0,1:T(8,128)(2,1)S(1)}, u32[]{:S(2)}, u32[]{:S(2)}) collective-permute-start(bf16[8,2,8,1024]{3,2,0,1:T(8,128)(2,1)S(1)} %fusion.12), channel_id=1, source_target_pairs={{4,0},{5,1},{6,2},{7,3},{8,12},{9,13},{10,14},{11,15},{20,16},{21,... | collective-permute-start | bytes 786440 | tf_op jit(solution)/shard_map/ppermute | solution.py:27
  254.8 17.9 %all-to-all-start.2 = ((bf16[8,8,8,1024]{3,2,1,0:T(8,128)(2,1)}), bf16[8,8,8,1024]{3,2,1,0:T(8,128)(2,1)S(1)}, u32[]{:S(2)}, u32[]{:S(2)}) async-start(bf16[8,8,8,1024]{3,2,1,0:T(8,128)(2,1)} %copy.30), calls=%async_computation.2 | async-start | bytes 2097152 | tf_op jit(solution)/shard_map/all_to_all | solution.py:30
  286.9 16.3 %copy-start.1 = (bf16[4,64,1024]{2,1,0:T(8,128)(2,1)S(1)}, bf16[4,64,1024]{2,1,0:T(8,128)(2,1)}, u32[]{:S(2)}) copy-start(bf16[4,64,1024]{2,1,0:T(8,128)(2,1)} %param.9) | copy-start | bytes 1572868
Sparse Core Ops, SparseCore 0:
  9.5 160.0 all-gather.2

commit v3 on v2

--- a/solution.py
+++ b/solution.py
@@ -19,8 +19,6 @@
         [r * devices + z * inner + j for r in range(reps) for j in range(inner)]
         for z in range(layers)
     ]
-    same_core = [list(range(c, devices, 2)) for c in range(2)]
-    core_swap = [(i, i ^ 1) for i in range(devices)]
 
     def hop(array, *pairs):
         moves = [(a * inner + j, b * inner + j) for a, b in pairs for j in range(inner)]
@@ -42,13 +40,24 @@
     def after(array, earlier):
         return lax.optimization_barrier((array, earlier))[0]
 
-    def whole_value(value_weight, earlier):
-        mine = lax.all_gather(value_weight, "ad", axis=0, tiled=False, axis_index_groups=same_core)
-        mine = after(mine, earlier)
-        other = lax.ppermute(mine, "ad", core_swap)
-        first = lax.axis_index("ad") % 2 == 0
-        both = jnp.stack([jnp.where(first, mine, other), jnp.where(first, other, mine)], axis=1)
-        return both.reshape(-1, value_weight.shape[1])
+    def swapped(array, bit):
+        return lax.ppermute(array, "ad", [(i, i ^ bit) for i in range(devices)])
+
+    def based(tokens, value_weight, earlier):
+        depth = value_weight.shape[0]
+        held = lax.all_gather(value_weight, "ad", axis=0, tiled=True, axis_index_groups=columns)
+        held = after(held, earlier)
+        pieces = {0: held}
+        for bit in [1 << k for k in reversed(range(inner.bit_length() - 1))]:
+            pieces.update({at ^ bit: swapped(piece, bit) for at, piece in list(pieces.items())})
+        lane = lax.axis_index("ad") % inner
+        columned = tokens.reshape(tokens.shape[0], layers, inner, depth)
+        total = 0
+        for at in sorted(pieces, key=lambda at: (at > 1, at)):
+            part = lax.dynamic_slice_in_dim(columned, lane ^ at, 1, 2)
+            part = part.reshape(tokens.shape[0], layers * depth)
+            total = total + jnp.dot(part, pieces[at], preferred_element_type=F32)
+        return total
 
     def on_device(tokens, value_weight, down_weight, up_weight, request_adapter, adapter_home_slot):
         rows, model_width = tokens.shape
@@ -115,7 +124,7 @@
             crossed = hop(pair, (1, 2), (2, 1))
             outer = hop(mid, (1, 0), (2, 3))
             extra_rows = hop(far_rows, (0, 1), (3, 2))
-            base = jnp.dot(tokens, whole_value(value_weight, near_sent), preferred_element_type=F32)
+            base = based(tokens, value_weight, far_rows)
             extra = hop(adapt(extra_rows, crossed, model_width), (1, 0), (2, 3))
             far = jnp.where(edge, extra, adapt(far_rows, crossed, model_width))
             panels = jnp.concatenate([own, pair, jnp.where(edge, outer, mid)], axis=0)
@@ -125,7 +134,7 @@
             sent = outgoing(0, layers)
             incoming = exchange(sent)
             panels = lax.all_gather(own, "ad", axis=0, tiled=True, axis_index_groups=columns)
-            base = jnp.dot(tokens, whole_value(value_weight, sent), preferred_element_type=F32)
+            base = based(tokens, value_weight, sent)
             back = exchange(adapt(incoming, panels, model_width))
         return (base + delta(back, 0, layers)).astype(BF16)
 

time: 313 us -> 360 us (1.15)
  waiting for transfers between devices: 198 us -> 230 us
  local copies, waits for them, and re-layouts: 7.55 us -> 24.7 us
  other arithmetic: 18.7 us -> 6.62 us
  matrix products: 43.4 us -> 49.7 us
  starting transfers between devices: 28.8 us -> 32.7 us
    all_gather x1, waiting for transfers between devices: 135 us -> 0.01 us  [based(): lax.all_gather(value_weight, 'ad', axis=0, tiled=True, axis_index_groups=...]
    ppermute x1 -> x3, waiting for transfers between devices: 0.01 us -> 94.9 us  [swapped(): return lax.ppermute(array, 'ad', [(i, i ^ bit) for i in range(devices)])]
    ppermute x6, waiting for transfers between devices: 45.9 us -> 130 us  [hop(): return lax.ppermute(array, 'ad', moves)]
    another operation x2 -> x0, other arithmetic: 13.2 us -> none  [whole_value(): jnp.stack([jnp.where(first, mine, other), jnp.where(first, other, mine)],...]
    unnamed x8 -> x17, local copies, waits for them, and re-layouts: 0.33 us -> 12.3 us
    all_to_all x3, waiting for transfers between devices: 16.1 us -> 4.11 us  [exchange(): lax.all_to_all(array, ('rep', 'ad'), split_axis=0, concat_axis=0, tiled=T...]
    dynamic_slice x0 -> x1, local copies, waits for them, and re-layouts: none -> 6.48 us  [based(): part = lax.dynamic_slice_in_dim(columned, lane ^ at, 1, 2)]
    dot_general x1 -> x4, matrix products: 14.9 us -> 18.7 us  [based(): total = total + jnp.dot(part, pieces[at], preferred_element_type=F32)]
  transfers between devices with their start and end apart: 11 -> 13, of which waited for: 5 -> 5; matrix products, arithmetic and copies ran while one was open for 13% -> 21% of each run, Pallas kernels for 0% -> 0%
where the time goes in v3:
time: 360 us; the launch traced here: 357 us
  waiting for transfers between devices  230 us (64%)
  matrix products  49.7 us (14%)
  starting transfers between devices  32.7 us (9%)
  local copies, waits for them, and re-layouts  24.7 us (7%)
  between operations  13.7 us (4%)
  other arithmetic  6.62 us (2%)
    ppermute x6, waiting for transfers between devices, hop(): return lax.ppermute(array, 'ad', moves)  130 us
    ppermute x3, waiting for transfers between devices, swapped(): return lax.ppermute(array, 'ad', [(i, i ^ bit) for i in range(devices)])  94.9 us
    dot_general x4, matrix products, based(): total = total + jnp.dot(part, pieces[at], preferred_element_type=F32)  18.7 us
    ppermute x6, starting transfers between devices, hop(): return lax.ppermute(array, 'ad', moves)  17.2 us
    dot_general x2, matrix products, outgoing(): sent = jnp.dot(pick, tokens, preferred_element_type=F32).astype(BF16)  15.3 us
    all_to_all x3, starting transfers between devices, exchange(): lax.all_to_all(array, ('rep', 'ad'), split_axis=0, concat_axis=0, tiled=T...  13.6 us
    dot_general x3, matrix products, adapt(): jnp.einsum('sajr,arn->sajn', latent, panel[:, :, model_width:], preferred...  13.5 us
    unnamed x17, local copies, waits for them, and re-layouts  12.3 us
  transfers between devices with their start and end apart: 13, of which 5 were waited for; matrix products, arithmetic and copies ran while one was open for 21% of the time, Pallas kernels for 0%

profile of v3, /device:TPU:8, one launch (start us, length us, event | category | flops | bytes accessed | tf_op | source)
XLA Modules:
  0.0 357.1 jit_solution(7835522527044943883)
XLA Ops:
  6.5 0.0 copy-start
  6.5 0.0 all-gather.2.cloned.1.call-start
  6.5 0.7 all-gather.2.cloned.1.call-update
  7.3 0.3 copy-done
  7.6 1.7 dynamic-slice_bitcast_fusion
  9.3 0.0 copy-start.5
  9.3 0.0 copy-start.6
  9.4 1.6 pad_maximum_fusion.5
  11.0 3.5 collective-permute-start.4
  14.5 0.1 collective-permute-start.3
  14.6 0.0 copy-done.5
  14.6 0.0 copy-done.6
  14.6 0.1 select_reduce_fusion
  14.7 0.3 convert_reduce_fusion
  15.0 6.5 %convolution_convert_fusion.1 = bf16[128,8192]{1,0:T(8,128)(2,1)} fusion(bf16[512,8192]{1,0:T(8,128)(2,1)} %param.6, s32[512]{0:T(512)S(1)} %fusion.60, s32[128]{0:T(128)S(1)} %fusion.93), kind=kOutput, calls=%fused_computation.1 | convolution fusion | flops 1074855936 | bytes 10488320 | tf_op jit(solution)/shard_map/dot_general | solution.py:107
  21.5 4.3 %all-to-all-start = ((bf16[8,2,8,8192]{3,2,1,0:T(8,128)(2,1)}), bf16[8,2,8,8192]{3,2,1,0:T(8,128)(2,1)}, u32[]{:S(2)}, u32[]{:S(2)}) async-start(bf16[8,2,8,8192]{3,2,1,0:T(8,128)(2,1)} %bitcast.82), calls=%async_computation | async-start | bytes 4194304 | tf_op jit(solution)/shard_map/all_to_all | solution.py:28
  25.8 8.9 %convolution_convert_fusion = bf16[384,8192]{1,0:T(8,128)(2,1)} fusion(bf16[512,8192]{1,0:T(8,128)(2,1)} %param.6, s32[512]{0:T(512)S(1)} %fusion.60, s32[384]{0:T(512)S(1)} %fusion.69), kind=kOutput, calls=%fused_computation | convolution fusion | flops 3224567808 | bytes 14683648 | tf_op jit(solution)/shard_map/dot_general | solution.py:107
  34.7 98.1 %collective-permute-done.3 = bf16[2,64,9216]{2,1,0:T(8,128)(2,1)} collective-permute-done((bf16[2,64,9216]{2,1,0:T(8,128)(2,1)}, bf16[2,64,9216]{2,1,0:T(8,128)(2,1)}, u32[]{:S(2)}, u32[]{:S(2)}) %collective-permute-start.3) | collective-permute-done | bytes 2359328 | tf_op jit(solution)/shard_map/ppermute | solution.py:25
  132.8 3.5 collective-permute-start.6
  136.3 0.0 all-to-all-done
  136.3 4.8 %all-to-all-start.1 = ((bf16[8,6,8,8192]{3,2,1,0:T(8,128)(2,1)}), bf16[8,6,8,8192]{3,2,1,0:T(8,128)(2,1)}, u32[]{:S(2)}, u32[]{:S(2)}) async-start(bf16[8,6,8,8192]{3,2,1,0:T(8,128)(2,1)} %bitcast.83), calls=%async_computation.1 | async-start | bytes 12582912 | tf_op jit(solution)/shard_map/all_to_all | solution.py:28
  141.1 3.1 copy.19
  144.2 1.3 collective-permute-start.7
  145.5 0.0 collective-permute-done.4
  145.5 7.4 %collective-permute-start.5 = (bf16[2,64,9216]{2,1,0:T(8,128)(2,1)}, bf16[2,64,9216]{2,1,0:T(8,128)(2,1)}, u32[]{:S(2)}, u32[]{:S(2)}) collective-permute-start(bf16[2,64,9216]{2,1,0:T(8,128)(2,1)} %collective-permute-done.4), channel_id=1, source_target_pairs={{4,0},{5,1},{6,2},{7,3},{8,12},{9,13},{10,14},{11,15},{20,16},{21,... | collective-permute-start | bytes 7077896 | tf_op jit(solution)/shard_map/ppermute | solution.py:25
  152.9 0.0 all-gather.2.cloned.1.call-done
  152.9 1.9 collective-permute-start.1
  154.8 12.0 %copy.17 = bf16[512,8192]{0,1:T(8,128)(2,1)} copy(bf16[512,8192]{1,0:T(8,128)(2,1)} %param.6) | data formatting | bytes 16777216 | tf_op args[0]
  166.8 27.6 %collective-permute-done.7 = bf16[8,2,8,8192]{3,2,0,1:T(8,128)(2,1)} collective-permute-done((bf16[8,2,8,8192]{3,2,0,1:T(8,128)(2,1)}, bf16[8,2,8,8192]{3,2,0,1:T(8,128)(2,1)}, u32[]{:S(2)}, u32[]{:S(2)}) %collective-permute-start.7) | collective-permute-done | bytes 2097184 | tf_op jit(solution)/shard_map/ppermute | solution.py:25
  194.3 0.0 collective-permute-done.6
  194.3 3.2 fusion.11
  197.5 1.5 collective-permute-start.8
  199.0 0.1 collective-permute-start
  199.1 4.3 %collective-permute-done.5 = bf16[2,64,9216]{2,1,0:T(8,128)(2,1)} collective-permute-done((bf16[2,64,9216]{2,1,0:T(8,128)(2,1)}, bf16[2,64,9216]{2,1,0:T(8,128)(2,1)}, u32[]{:S(2)}, u32[]{:S(2)}) %collective-permute-start.5) | collective-permute-done | bytes 2359328 | tf_op jit(solution)/shard_map/ppermute | solution.py:25
  203.3 3.3 broadcast_select_fusion
  206.7 94.9 %collective-permute-done.1 = bf16[2048,1024]{1,0:T(8,128)(2,1)} collective-permute-done((bf16[2048,1024]{1,0:T(8,128)(2,1)}, bf16[2048,1024]{1,0:T(8,128)(2,1)}, u32[]{:S(2)}, u32[]{:S(2)}) %collective-permute-start.1) | collective-permute-done | bytes 4194336 | tf_op jit(solution)/shard_map/ppermute | solution.py:44
  301.6 0.0 collective-permute-start.2
  301.6 3.2 fusion.10
  304.8 0.0 collective-permute-done.8
  304.9 0.0 all-to-all-done.1
  304.9 7.1 %fusion.7 = bf16[8,6,8,1024]{3,2,0,1:T(8,128)(2,1)} fusion(bf16[8,6,8,8192]{3,2,1,0:T(8,128)(2,1)} %all-to-all-done.1, bf16[2,64,9216]{2,1,0:T(8,128)(2,1)} %broadcast_select_fusion, bf16[2,64,9216]{2,1,0:T(8,128)(2,1)} %collective-permute-done.3, bf16[2,64,1024]{2,1,0:T(8,128)(2,1)S(1)} %constant_dynamic-slice_fusion, ...), kind=kOutput, calls=%fused_computation.17 | convolution fusion | flops 482107392 | bytes 14155776 | tf_op jit(solution)/shard_map/sajr,arn->sajn/dot_general | solution.py:37
  312.0 1.2 pad_maximum_fusion.6
  313.2 1.1 copy.21
  314.3 4.4 %all-to-all-start.2 = ((bf16[8,8,8,1024]{3,2,1,0:T(8,128)(2,1)}), bf16[8,8,8,1024]{3,2,1,0:T(8,128)(2,1)}, u32[]{:S(2)}, u32[]{:S(2)}) async-start(bf16[8,8,8,1024]{3,2,1,0:T(8,128)(2,1)} %copy.21), calls=%async_computation.2 | async-start | bytes 2097152 | tf_op jit(solution)/shard_map/all_to_all | solution.py:28
  318.7 0.0 copy-start.7
  318.7 6.5 %constant_dynamic-slice_fusion.1 = (bf16[512,4,1,512]{0,3,2,1:T(8,128)(2,1)S(1)}, bf16[512,4,1,512]{0,3,2,1:T(8,128)(2,1)}, bf16[512,4,1,512]{0,3,2,1:T(8,128)(2,1)}, bf16[512,4,1,512]{0,3,2,1:T(8,128)(2,1)S(1)}) fusion(bf16[512,4,4,512]{0,3,2,1:T(8,128)(2,1)} %bitcast.80, s32[]{:T(128)S(6)} %select_n.274, s32[]{:T(128)S(6)} %select_n.273, ...), kind=kLoop, calls=%fused_computation.137 | loop fusion | bytes 16777232 | tf_op jit(solution)/shard_map/dynamic_slice | solution.py:57
  325.2 0.0 copy-done.7
  325.2 3.7 %fusion.100 = f32[512,1024]{1,0:T(8,128)} fusion(bf16[512,2048]{0,1:T(8,128)(2,1)S(1)} %bitcast.86, bf16[2048,1024]{1,0:T(8,128)(2,1)S(1)} %copy-done.7), kind=kOutput, calls=%fused_computation.149 | convolution fusion | flops 2147483648 | bytes 8388608 | tf_op jit(solution)/shard_map/dot_general | solution.py:59
  328.9 4.1 %all-to-all-done.2 = bf16[8,8,8,1024]{3,2,1,0:T(8,128)(2,1)} async-done(((bf16[8,8,8,1024]{3,2,1,0:T(8,128)(2,1)}), bf16[8,8,8,1024]{3,2,1,0:T(8,128)(2,1)}, u32[]{:S(2)}, u32[]{:S(2)}) %all-to-all-start.2) | async-done | bytes 1048608 | tf_op jit(solution)/shard_map/all_to_all | solution.py:28
  333.0 0.0 copy-start.4
  333.0 2.1 fusion.31
  335.1 0.0 copy-done.4
  335.1 0.0 copy-start.3
  335.1 4.7 %fusion.102 = f32[512,1024]{1,0:T(8,128)S(1)} fusion(bf16[512,2048]{0,1:T(8,128)(2,1)S(1)} %bitcast.85, bf16[2048,1024]{1,0:T(8,128)(2,1)} %collective-permute-done.1), kind=kOutput, calls=%fused_computation.151 | convolution fusion | flops 2147483648 | bytes 8388608 | tf_op jit(solution)/shard_map/dot_general | solution.py:59
  339.8 0.0 collective-permute-done
  339.8 0.0 copy-done.3
  339.8 0.0 copy-start.2
  339.8 4.7 %fusion.101 = f32[512,1024]{1,0:T(8,128)S(1)} fusion(bf16[512,2048]{0,1:T(8,128)(2,1)S(1)} %bitcast.84, bf16[2048,1024]{1,0:T(8,128)(2,1)} %collective-permute-done), kind=kOutput, calls=%fused_computation.150 | convolution fusion | flops 2147483648 | bytes 8388608 | tf_op jit(solution)/shard_map/dot_general | solution.py:59
  344.5 0.0 collective-permute-done.2
  344.5 0.0 copy-done.2
  344.5 0.0 copy-start.1
  344.6 5.7 %add_convert_fusion = bf16[512,1024]{1,0:T(8,128)(2,1)} fusion(f32[512,1024]{1,0:T(8,128)S(1)} %fusion.31, f32[512,1024]{1,0:T(8,128)S(1)} %fusion.102, f32[512,1024]{1,0:T(8,128)S(1)} %copy-done.2, f32[512,1024]{1,0:T(8,128)S(1)} %fusion.101, bf16[512,2048]{0,1:T(8,128)(2,1)S(1)} %bitcast.81, bf16[2048,1024]{1,0:T(8,128)(2,1)} %collective-permute-done.2), kind=kOutput, calls=%fused_computation.12 | convolution fusion | flops 2150105088 | bytes 15728640 | tf_op jit(solution)/shard_map/dot_general | solution.py:59
  350.3 0.0 copy-done.1
  (6 shorter events, 0.1 us)
Async XLA Ops:
  6.5 1.0 copy-start
  6.5 146.3 %all-gather.2.cloned.1.call-start = ((), (), s32[]{:S(2)}) async-start(), calls=%async_computation.3 | async-start | bytes 5242880 | tf_op jit(solution)/shard_map/all_gather | solution.py:48
  9.3 5.2 %copy-start.5 = (s32[512]{0:T(512)S(1)}, s32[512]{0:T(512)}, u32[]{:S(2)}) copy-start(s32[512]{0:T(512)} %param.10) | copy-start | bytes 6148
  9.3 5.2 %copy-start.6 = (s32[64]{0:T(128)S(1)}, s32[64]{0:T(128)}, u32[]{:S(2)}) copy-start(s32[64]{0:T(128)} %param.11) | copy-start | bytes 772
  11.0 134.5 %collective-permute-start.4 = (bf16[2,64,9216]{2,1,0:T(8,128)(2,1)}, bf16[2,64,9216]{2,1,0:T(8,128)(2,1)}, u32[]{:S(2)}, u32[]{:S(2)}) collective-permute-start(bf16[2,64,9216]{2,1,0:T(8,128)(2,1)} %pad_maximum_fusion.5), channel_id=1, source_target_pairs={{4,8},{5,9},{6,10},{7,11},{8,4},{9,5},{10,6},{11,7},{20,24},{21,25... | collective-permute-start | bytes 7077896 | tf_op jit(solution)/shard_map/ppermute | solution.py:25
  14.5 118.3 %collective-permute-start.3 = (bf16[2,64,9216]{2,1,0:T(8,128)(2,1)}, bf16[2,64,9216]{2,1,0:T(8,128)(2,1)}, u32[]{:S(2)}, u32[]{:S(2)}) collective-permute-start(bf16[2,64,9216]{2,1,0:T(8,128)(2,1)} %pad_maximum_fusion.5), channel_id=1, source_target_pairs={{0,4},{1,5},{2,6},{3,7},{4,0},{5,1},{6,2},{7,3},{8,12},{9,13},{10,... | collective-permute-start | bytes 7077896 | tf_op jit(solution)/shard_map/ppermute | solution.py:25
  21.5 114.9 %all-to-all-start = ((bf16[8,2,8,8192]{3,2,1,0:T(8,128)(2,1)}), bf16[8,2,8,8192]{3,2,1,0:T(8,128)(2,1)}, u32[]{:S(2)}, u32[]{:S(2)}) async-start(bf16[8,2,8,8192]{3,2,1,0:T(8,128)(2,1)} %bitcast.82), calls=%async_computation | async-start | bytes 4194304 | tf_op jit(solution)/shard_map/all_to_all | solution.py:28
  132.8 61.6 %collective-permute-start.6 = (bf16[2,64,9216]{2,1,0:T(8,128)(2,1)}, bf16[2,64,9216]{2,1,0:T(8,128)(2,1)}, u32[]{:S(2)}, u32[]{:S(2)}) collective-permute-start(bf16[2,64,9216]{2,1,0:T(8,128)(2,1)} %collective-permute-done.3), channel_id=1, source_target_pairs={{4,8},{5,9},{6,10},{7,11},{8,4},{9,5},{10,6},{11,7},{20,24},{21,25... | collective-permute-start | bytes 7077896 | tf_op jit(solution)/shard_map/ppermute | solution.py:25
  136.3 168.5 %all-to-all-start.1 = ((bf16[8,6,8,8192]{3,2,1,0:T(8,128)(2,1)}), bf16[8,6,8,8192]{3,2,1,0:T(8,128)(2,1)}, u32[]{:S(2)}, u32[]{:S(2)}) async-start(bf16[8,6,8,8192]{3,2,1,0:T(8,128)(2,1)} %bitcast.83), calls=%async_computation.1 | async-start | bytes 12582912 | tf_op jit(solution)/shard_map/all_to_all | solution.py:28
  144.2 50.1 %collective-permute-start.7 = (bf16[8,2,8,8192]{3,2,0,1:T(8,128)(2,1)}, bf16[8,2,8,8192]{3,2,0,1:T(8,128)(2,1)}, u32[]{:S(2)}, u32[]{:S(2)}) collective-permute-start(bf16[8,2,8,8192]{3,2,0,1:T(8,128)(2,1)} %copy.19), channel_id=1, source_target_pairs={{0,4},{1,5},{2,6},{3,7},{12,8},{13,9},{14,10},{15,11},{16,20},{17,... | collective-permute-start | bytes 6291464 | tf_op jit(solution)/shard_map/ppermute | solution.py:25
  145.5 57.8 %collective-permute-start.5 = (bf16[2,64,9216]{2,1,0:T(8,128)(2,1)}, bf16[2,64,9216]{2,1,0:T(8,128)(2,1)}, u32[]{:S(2)}, u32[]{:S(2)}) collective-permute-start(bf16[2,64,9216]{2,1,0:T(8,128)(2,1)} %collective-permute-done.4), channel_id=1, source_target_pairs={{4,0},{5,1},{6,2},{7,3},{8,12},{9,13},{10,14},{11,15},{20,16},{21,... | collective-permute-start | bytes 7077896 | tf_op jit(solution)/shard_map/ppermute | solution.py:25
  152.9 148.7 %collective-permute-start.1 = (bf16[2048,1024]{1,0:T(8,128)(2,1)}, bf16[2048,1024]{1,0:T(8,128)(2,1)}, u32[]{:S(2)}, u32[]{:S(2)}) collective-permute-start(bf16[2048,1024]{1,0:T(8,128)(2,1)} %all-gather.2.cloned.1.call-done), channel_id=1, source_target_pairs={{0,2},{1,3},{2,0},{3,1},{4,6},{5,7},{6,4},{7,5},{8,10},{9,11},{10,... | collective-permute-start | bytes 12582920 | tf_op jit(solution)/shard_map/ppermute | solution.py:44
  197.5 107.3 %collective-permute-start.8 = (bf16[8,2,8,1024]{3,2,0,1:T(8,128)(2,1)S(1)}, bf16[8,2,8,1024]{3,2,0,1:T(8,128)(2,1)S(1)}, u32[]{:S(2)}, u32[]{:S(2)}) collective-permute-start(bf16[8,2,8,1024]{3,2,0,1:T(8,128)(2,1)S(1)} %fusion.11), channel_id=1, source_target_pairs={{4,0},{5,1},{6,2},{7,3},{8,12},{9,13},{10,14},{11,15},{20,16},{21,... | collective-permute-start | bytes 786440 | tf_op jit(solution)/shard_map/ppermute | solution.py:25
  199.0 140.8 %collective-permute-start = (bf16[2048,1024]{1,0:T(8,128)(2,1)}, bf16[2048,1024]{1,0:T(8,128)(2,1)}, u32[]{:S(2)}, u32[]{:S(2)}) collective-permute-start(bf16[2048,1024]{1,0:T(8,128)(2,1)} %all-gather.2.cloned.1.call-done), channel_id=1, source_target_pairs={{0,1},{1,0},{2,3},{3,2},{4,5},{5,4},{6,7},{7,6},{8,9},{9,8},{10,11... | collective-permute-start | bytes 12582920 | tf_op jit(solution)/shard_map/ppermute | solution.py:44
  301.6 42.9 %collective-permute-start.2 = (bf16[2048,1024]{1,0:T(8,128)(2,1)}, bf16[2048,1024]{1,0:T(8,128)(2,1)}, u32[]{:S(2)}, u32[]{:S(2)}) collective-permute-start(bf16[2048,1024]{1,0:T(8,128)(2,1)} %collective-permute-done.1), channel_id=1, source_target_pairs={{0,1},{1,0},{2,3},{3,2},{4,5},{5,4},{6,7},{7,6},{8,9},{9,8},{10,11... | collective-permute-start | bytes 12582920 | tf_op jit(solution)/shard_map/ppermute | solution.py:44
  314.3 18.7 %all-to-all-start.2 = ((bf16[8,8,8,1024]{3,2,1,0:T(8,128)(2,1)}), bf16[8,8,8,1024]{3,2,1,0:T(8,128)(2,1)}, u32[]{:S(2)}, u32[]{:S(2)}) async-start(bf16[8,8,8,1024]{3,2,1,0:T(8,128)(2,1)} %copy.21), calls=%async_computation.2 | async-start | bytes 2097152 | tf_op jit(solution)/shard_map/all_to_all | solution.py:28
  318.7 6.5 %copy-start.7 = (bf16[2048,1024]{1,0:T(8,128)(2,1)S(1)}, bf16[2048,1024]{1,0:T(8,128)(2,1)}, u32[]{:S(2)}) copy-start(bf16[2048,1024]{1,0:T(8,128)(2,1)} %all-gather.2.cloned.1.call-done) | copy-start | bytes 12582916
  333.0 2.1 copy-start.4
  335.1 4.7 %copy-start.3 = (bf16[512,4,1,512]{0,3,2,1:T(8,128)(2,1)S(1)}, bf16[512,4,1,512]{0,3,2,1:T(8,128)(2,1)}, u32[]{:S(2)}) copy-start(bf16[512,4,1,512]{0,3,2,1:T(8,128)(2,1)} %get-tuple-element.13) | copy-start | bytes 6291460
  339.8 4.7 %copy-start.2 = (f32[512,1024]{1,0:T(8,128)S(1)}, f32[512,1024]{1,0:T(8,128)}, u32[]{:S(2)}) copy-start(f32[512,1024]{1,0:T(8,128)} %fusion.100) | copy-start | bytes 6291460
  344.5 5.7 %copy-start.1 = (bf16[4,64,1024]{2,1,0:T(8,128)(2,1)S(1)}, bf16[4,64,1024]{2,1,0:T(8,128)(2,1)}, u32[]{:S(2)}) copy-start(bf16[4,64,1024]{2,1,0:T(8,128)(2,1)} %param.9) | copy-start | bytes 1572868
Sparse Core Ops, SparseCore 0:
  8.9 126.3 all-gather.1

commit v4 on v2

--- a/solution.py
+++ b/solution.py
@@ -19,8 +19,6 @@
         [r * devices + z * inner + j for r in range(reps) for j in range(inner)]
         for z in range(layers)
     ]
-    same_core = [list(range(c, devices, 2)) for c in range(2)]
-    core_swap = [(i, i ^ 1) for i in range(devices)]
 
     def hop(array, *pairs):
         moves = [(a * inner + j, b * inner + j) for a, b in pairs for j in range(inner)]
@@ -41,14 +39,6 @@
 
     def after(array, earlier):
         return lax.optimization_barrier((array, earlier))[0]
-
-    def whole_value(value_weight, earlier):
-        mine = lax.all_gather(value_weight, "ad", axis=0, tiled=False, axis_index_groups=same_core)
-        mine = after(mine, earlier)
-        other = lax.ppermute(mine, "ad", core_swap)
-        first = lax.axis_index("ad") % 2 == 0
-        both = jnp.stack([jnp.where(first, mine, other), jnp.where(first, other, mine)], axis=1)
-        return both.reshape(-1, value_weight.shape[1])
 
     def on_device(tokens, value_weight, down_weight, up_weight, request_adapter, adapter_home_slot):
         rows, model_width = tokens.shape
@@ -110,12 +100,12 @@
             far_rows = exchange(outgoing(3, 1))
             near_sent = outgoing(0, 3)
             near_rows = exchange(near_sent)
-            pair = after(hop(own, (0, 1), (1, 0), (2, 3), (3, 2)), near_sent)
-            mid = after(hop(own, (1, 2), (2, 1)), near_sent)
+            pair = after(hop(own, (0, 1), (1, 0), (2, 3), (3, 2)), (far_rows, near_sent))
+            mid = after(hop(own, (1, 2), (2, 1)), (far_rows, near_sent))
             crossed = hop(pair, (1, 2), (2, 1))
             outer = hop(mid, (1, 0), (2, 3))
             extra_rows = hop(far_rows, (0, 1), (3, 2))
-            base = jnp.dot(tokens, whole_value(value_weight, near_sent), preferred_element_type=F32)
+            base = jnp.dot(tokens, lax.all_gather(value_weight, "ad", axis=0, tiled=True), preferred_element_type=F32)
             extra = hop(adapt(extra_rows, crossed, model_width), (1, 0), (2, 3))
             far = jnp.where(edge, extra, adapt(far_rows, crossed, model_width))
             panels = jnp.concatenate([own, pair, jnp.where(edge, outer, mid)], axis=0)
@@ -125,7 +115,7 @@
             sent = outgoing(0, layers)
             incoming = exchange(sent)
             panels = lax.all_gather(own, "ad", axis=0, tiled=True, axis_index_groups=columns)
-            base = jnp.dot(tokens, whole_value(value_weight, sent), preferred_element_type=F32)
+            base = jnp.dot(tokens, lax.all_gather(value_weight, "ad", axis=0, tiled=True), preferred_element_type=F32)
             back = exchange(adapt(incoming, panels, model_width))
         return (base + delta(back, 0, layers)).astype(BF16)
 

time: 313 us -> 275 us (0.88)
  waiting for transfers between devices: 198 us -> 166 us
  other arithmetic: 18.7 us -> 5.76 us
  starting transfers between devices: 28.8 us -> 32.3 us
    all_gather x1, waiting for transfers between devices: 135 us -> 0.01 us  [on_device(): lax.all_gather(value_weight, 'ad', axis=0, tiled=True)]
    ppermute x6, waiting for transfers between devices: 45.9 us -> 130 us  [hop(): return lax.ppermute(array, 'ad', moves)]
    all_to_all x3, waiting for transfers between devices: 16.1 us -> 35.7 us  [exchange(): lax.all_to_all(array, ('rep', 'ad'), split_axis=0, concat_axis=0, tiled=T...]
    another operation x2 -> x0, other arithmetic: 13.2 us -> none  [whole_value(): jnp.stack([jnp.where(first, mine, other), jnp.where(first, other, mine)],...]
  transfers between devices with their start and end apart: 11 -> 10, of which waited for: 5 -> 6; matrix products, arithmetic and copies ran while one was open for 13% -> 15% of each run, Pallas kernels for 0% -> 0%
where the time goes in v4:
time: 275 us; the launch traced here: 270 us
  waiting for transfers between devices  166 us (60%)
  matrix products  45.8 us (17%)
  starting transfers between devices  32.3 us (12%)
  between operations  13.6 us (5%)
  local copies, waits for them, and re-layouts  6.24 us (2%)
  other arithmetic  5.76 us (2%)
    ppermute x6, waiting for transfers between devices, hop(): return lax.ppermute(array, 'ad', moves)  130 us
    all_to_all x3, waiting for transfers between devices, exchange(): lax.all_to_all(array, ('rep', 'ad'), split_axis=0, concat_axis=0, tiled=T...  35.7 us
    ppermute x6, starting transfers between devices, hop(): return lax.ppermute(array, 'ad', moves)  17.1 us
    dot_general x1, matrix products, on_device(): jnp.dot(tokens, lax.all_gather(value_weight, 'ad', axis=0, tiled=True), p...  15.9 us
    all_to_all x3, starting transfers between devices, exchange(): lax.all_to_all(array, ('rep', 'ad'), split_axis=0, concat_axis=0, tiled=T...  15.2 us
    dot_general x2, matrix products, outgoing(): sent = jnp.dot(pick, tokens, preferred_element_type=F32).astype(BF16)  15 us
    dot_general x3, matrix products, adapt(): jnp.einsum('sajr,arn->sajn', latent, panel[:, :, model_width:], preferred...  12.8 us
  transfers between devices with their start and end apart: 10, of which 6 were waited for; matrix products, arithmetic and copies ran while one was open for 15% of the time, Pallas kernels for 0%

profile of v4, /device:TPU:8, one launch (start us, length us, event | category | flops | bytes accessed | tf_op | source)
XLA Modules:
  0.0 269.9 jit_solution(4084077117629140657)
XLA Ops:
  6.5 0.0 copy-start
  6.5 0.0 all-gather.2.cloned.1.call-start
  6.5 0.7 all-gather.2.cloned.1.call-update
  7.3 0.3 copy-done
  7.6 1.8 dynamic-slice_bitcast_fusion
  9.4 0.0 copy-start.2
  9.4 0.0 copy-start.3
  9.4 1.6 pad_maximum_fusion.5
  11.0 3.5 %collective-permute-start.1 = (bf16[2,64,9216]{2,1,0:T(8,128)(2,1)}, bf16[2,64,9216]{2,1,0:T(8,128)(2,1)}, u32[]{:S(2)}, u32[]{:S(2)}) collective-permute-start(bf16[2,64,9216]{2,1,0:T(8,128)(2,1)} %pad_maximum_fusion.5), channel_id=1, source_target_pairs={{4,8},{5,9},{6,10},{7,11},{8,4},{9,5},{10,6},{11,7},{20,24},{21,25... | collective-permute-start | bytes 7077896 | tf_op jit(solution)/shard_map/ppermute | solution.py:25
  14.5 0.1 collective-permute-start
  14.6 0.0 copy-done.2
  14.6 0.0 copy-done.3
  14.6 0.1 select_reduce_fusion
  14.7 0.3 convert_reduce_fusion
  15.0 6.1 %convolution_convert_fusion.1 = bf16[128,8192]{1,0:T(8,128)(2,1)} fusion(bf16[512,8192]{1,0:T(8,128)(2,1)} %param.6, s32[512]{0:T(512)S(1)} %fusion.60, s32[128]{0:T(128)S(1)} %fusion.93), kind=kOutput, calls=%fused_computation.1 | convolution fusion | flops 1074855936 | bytes 10488320 | tf_op jit(solution)/shard_map/dot_general | solution.py:88
  21.2 4.3 %all-to-all-start = ((bf16[8,2,8,8192]{3,2,1,0:T(8,128)(2,1)}), bf16[8,2,8,8192]{3,2,1,0:T(8,128)(2,1)}, u32[]{:S(2)}, u32[]{:S(2)}) async-start(bf16[8,2,8,8192]{3,2,1,0:T(8,128)(2,1)} %bitcast.69), calls=%async_computation | async-start | bytes 4194304 | tf_op jit(solution)/shard_map/all_to_all | solution.py:28
  25.5 8.8 %convolution_convert_fusion = bf16[384,8192]{1,0:T(8,128)(2,1)} fusion(bf16[512,8192]{1,0:T(8,128)(2,1)} %param.6, s32[512]{0:T(512)S(1)} %fusion.60, s32[384]{0:T(512)S(1)} %fusion.69), kind=kOutput, calls=%fused_computation | convolution fusion | flops 3224567808 | bytes 14683648 | tf_op jit(solution)/shard_map/dot_general | solution.py:88
  34.4 21.2 %all-to-all-done = bf16[8,2,8,8192]{3,2,1,0:T(8,128)(2,1)} async-done(((bf16[8,2,8,8192]{3,2,1,0:T(8,128)(2,1)}), bf16[8,2,8,8192]{3,2,1,0:T(8,128)(2,1)}, u32[]{:S(2)}, u32[]{:S(2)}) %all-to-all-start) | async-done | bytes 2097184 | tf_op jit(solution)/shard_map/all_to_all | solution.py:28
  55.6 52.0 %collective-permute-done = bf16[2,64,9216]{2,1,0:T(8,128)(2,1)} collective-permute-done((bf16[2,64,9216]{2,1,0:T(8,128)(2,1)}, bf16[2,64,9216]{2,1,0:T(8,128)(2,1)}, u32[]{:S(2)}, u32[]{:S(2)}) %collective-permute-start) | collective-permute-done | bytes 2359328 | tf_op jit(solution)/shard_map/ppermute | solution.py:25
  107.6 3.6 %collective-permute-start.3 = (bf16[2,64,9216]{2,1,0:T(8,128)(2,1)}, bf16[2,64,9216]{2,1,0:T(8,128)(2,1)}, u32[]{:S(2)}, u32[]{:S(2)}) collective-permute-start(bf16[2,64,9216]{2,1,0:T(8,128)(2,1)} %collective-permute-done), channel_id=1, source_target_pairs={{4,8},{5,9},{6,10},{7,11},{8,4},{9,5},{10,6},{11,7},{20,24},{21,25... | collective-permute-start | bytes 7077896 | tf_op jit(solution)/shard_map/ppermute | solution.py:25
  111.2 4.8 %all-to-all-start.1 = ((bf16[8,6,8,8192]{3,2,1,0:T(8,128)(2,1)}), bf16[8,6,8,8192]{3,2,1,0:T(8,128)(2,1)}, u32[]{:S(2)}, u32[]{:S(2)}) async-start(bf16[8,6,8,8192]{3,2,1,0:T(8,128)(2,1)} %bitcast.70), calls=%async_computation.1 | async-start | bytes 12582912 | tf_op jit(solution)/shard_map/all_to_all | solution.py:28
  116.0 3.1 %copy.16 = bf16[8,2,8,8192]{3,2,0,1:T(8,128)(2,1)} copy(bf16[8,2,8,8192]{3,2,1,0:T(8,128)(2,1)} %all-to-all-done) | data formatting | bytes 4194304 | tf_op jit(solution)/shard_map/all_to_all | solution.py:28
  119.1 1.3 collective-permute-start.4
  120.3 0.0 collective-permute-done.1
  120.4 7.3 %collective-permute-start.2 = (bf16[2,64,9216]{2,1,0:T(8,128)(2,1)}, bf16[2,64,9216]{2,1,0:T(8,128)(2,1)}, u32[]{:S(2)}, u32[]{:S(2)}) collective-permute-start(bf16[2,64,9216]{2,1,0:T(8,128)(2,1)} %collective-permute-done.1), channel_id=1, source_target_pairs={{4,0},{5,1},{6,2},{7,3},{8,12},{9,13},{10,14},{11,15},{20,16},{21,... | collective-permute-start | bytes 7077896 | tf_op jit(solution)/shard_map/ppermute | solution.py:25
  127.7 63.6 %collective-permute-done.4 = bf16[8,2,8,8192]{3,2,0,1:T(8,128)(2,1)} collective-permute-done((bf16[8,2,8,8192]{3,2,0,1:T(8,128)(2,1)}, bf16[8,2,8,8192]{3,2,0,1:T(8,128)(2,1)}, u32[]{:S(2)}, u32[]{:S(2)}) %collective-permute-start.4) | collective-permute-done | bytes 2097184 | tf_op jit(solution)/shard_map/ppermute | solution.py:25
  191.3 4.1 %collective-permute-done.3 = bf16[2,64,9216]{2,1,0:T(8,128)(2,1)} collective-permute-done((bf16[2,64,9216]{2,1,0:T(8,128)(2,1)}, bf16[2,64,9216]{2,1,0:T(8,128)(2,1)}, u32[]{:S(2)}, u32[]{:S(2)}) %collective-permute-start.3) | collective-permute-done | bytes 2359328 | tf_op jit(solution)/shard_map/ppermute | solution.py:25
  195.4 3.2 %fusion.11 = bf16[8,2,8,1024]{3,2,0,1:T(8,128)(2,1)S(1)} fusion(bf16[8,2,8,8192]{3,2,0,1:T(8,128)(2,1)} %collective-permute-done.4, bf16[2,64,9216]{2,1,0:T(8,128)(2,1)} %collective-permute-done.3), kind=kOutput, calls=%fused_computation.23 | convolution fusion | flops 151265280 | bytes 4718592 | tf_op jit(solution)/shard_map/sajr,arn->sajn/dot_general | solution.py:37
  198.6 1.3 collective-permute-start.5
  199.9 0.0 collective-permute-done.2
  199.9 3.6 %broadcast_select_fusion = bf16[2,64,9216]{2,1,0:T(8,128)(2,1)} fusion(bf16[2,64,9216]{2,1,0:T(8,128)(2,1)} %collective-permute-done.2, bf16[2,64,9216]{2,1,0:T(8,128)(2,1)} %collective-permute-done.1, pred[]{:T(512)S(6)} %or.3), kind=kLoop, calls=%fused_computation.10 | loop fusion | flops 1179648 | bytes 7077889 | tf_op jit(solution)/shard_map/jit(_where)/select_n | solution.py:111
  203.5 3.2 %fusion.10 = bf16[8,2,8,1024]{3,2,0,1:T(8,128)(2,1)S(1)} fusion(bf16[2,64,9216]{2,1,0:T(8,128)(2,1)} %collective-permute-done.3, bf16[8,2,8,8192]{3,2,1,0:T(8,128)(2,1)} %all-to-all-done), kind=kOutput, calls=%fused_computation.22 | convolution fusion | flops 151265280 | bytes 4718592 | tf_op jit(solution)/shard_map/sajr,arn->sajn/dot_general | solution.py:37
  206.7 10.1 %collective-permute-done.5 = bf16[8,2,8,1024]{3,2,0,1:T(8,128)(2,1)S(1)} collective-permute-done((bf16[8,2,8,1024]{3,2,0,1:T(8,128)(2,1)S(1)}, bf16[8,2,8,1024]{3,2,0,1:T(8,128)(2,1)S(1)}, u32[]{:S(2)}, u32[]{:S(2)}) %collective-permute-start.5) | collective-permute-done | bytes 262176 | tf_op jit(solution)/shard_map/ppermute | solution.py:25
  216.9 0.0 all-to-all-done.1
  216.9 6.5 %fusion.7 = bf16[8,6,8,1024]{3,2,0,1:T(8,128)(2,1)S(1)} fusion(bf16[8,6,8,8192]{3,2,1,0:T(8,128)(2,1)} %all-to-all-done.1, bf16[2,64,9216]{2,1,0:T(8,128)(2,1)} %broadcast_select_fusion, bf16[2,64,9216]{2,1,0:T(8,128)(2,1)} %collective-permute-done, bf16[2,64,1024]{2,1,0:T(8,128)(2,1)S(1)} %constant_dynamic-slice_fusion, ...), kind=kOutput, calls=%fused_computation.17 | convolution fusion | flops 482107392 | bytes 14155776 | tf_op jit(solution)/shard_map/sajr,arn->sajn/dot_general | solution.py:37
  223.4 0.1 pad_maximum_fusion.6
  223.5 1.1 copy.18
  224.5 6.1 %all-to-all-start.2 = ((bf16[8,8,8,1024]{3,2,1,0:T(8,128)(2,1)}), bf16[8,8,8,1024]{3,2,1,0:T(8,128)(2,1)S(1)}, u32[]{:S(2)}, u32[]{:S(2)}) async-start(bf16[8,8,8,1024]{3,2,1,0:T(8,128)(2,1)} %copy.18), calls=%async_computation.2 | async-start | bytes 2097152 | tf_op jit(solution)/shard_map/all_to_all | solution.py:28
  230.6 14.5 %all-to-all-done.2 = bf16[8,8,8,1024]{3,2,1,0:T(8,128)(2,1)S(1)} async-done(((bf16[8,8,8,1024]{3,2,1,0:T(8,128)(2,1)}), bf16[8,8,8,1024]{3,2,1,0:T(8,128)(2,1)S(1)}, u32[]{:S(2)}, u32[]{:S(2)}) %all-to-all-start.2) | async-done | bytes 1048608 | tf_op jit(solution)/shard_map/all_to_all | solution.py:28
  245.1 2.1 fusion.31
  247.1 0.0 all-gather.2.cloned.1.call-done
  247.1 0.0 copy-start.1
  247.1 15.9 %add_convert_fusion = bf16[512,1024]{1,0:T(8,128)(2,1)} fusion(f32[512,1024]{1,0:T(8,128)} %fusion.31, bf16[512,8192]{1,0:T(8,128)(2,1)} %param.6, bf16[8192,1024]{1,0:T(8,128)(2,1)} %all-gather.2.cloned.1.call-done), kind=kOutput, calls=%fused_computation.12 | convolution fusion | flops 8590983168 | bytes 28311552 | tf_op jit(solution)/shard_map/dot_general | solution.py:108
  263.1 0.0 copy-done.1
  (6 shorter events, 0.1 us)
Async XLA Ops:
  6.5 1.0 copy-start
  6.5 240.6 %all-gather.2.cloned.1.call-start = ((), (), s32[]{:S(2)}) async-start(), calls=%async_computation.3 | async-start | bytes 17825792 | tf_op jit(solution)/shard_map/all_gather | solution.py:108
  9.4 5.2 %copy-start.2 = (s32[512]{0:T(512)S(1)}, s32[512]{0:T(512)}, u32[]{:S(2)}) copy-start(s32[512]{0:T(512)} %param.10) | copy-start | bytes 6148
  9.4 5.2 %copy-start.3 = (s32[64]{0:T(128)S(1)}, s32[64]{0:T(128)}, u32[]{:S(2)}) copy-start(s32[64]{0:T(128)} %param.11) | copy-start | bytes 772
  11.0 109.3 %collective-permute-start.1 = (bf16[2,64,9216]{2,1,0:T(8,128)(2,1)}, bf16[2,64,9216]{2,1,0:T(8,128)(2,1)}, u32[]{:S(2)}, u32[]{:S(2)}) collective-permute-start(bf16[2,64,9216]{2,1,0:T(8,128)(2,1)} %pad_maximum_fusion.5), channel_id=1, source_target_pairs={{4,8},{5,9},{6,10},{7,11},{8,4},{9,5},{10,6},{11,7},{20,24},{21,25... | collective-permute-start | bytes 7077896 | tf_op jit(solution)/shard_map/ppermute | solution.py:25
  14.5 93.1 %collective-permute-start = (bf16[2,64,9216]{2,1,0:T(8,128)(2,1)}, bf16[2,64,9216]{2,1,0:T(8,128)(2,1)}, u32[]{:S(2)}, u32[]{:S(2)}) collective-permute-start(bf16[2,64,9216]{2,1,0:T(8,128)(2,1)} %pad_maximum_fusion.5), channel_id=1, source_target_pairs={{0,4},{1,5},{2,6},{3,7},{4,0},{5,1},{6,2},{7,3},{8,12},{9,13},{10,... | collective-permute-start | bytes 7077896 | tf_op jit(solution)/shard_map/ppermute | solution.py:25
  21.2 34.4 %all-to-all-start = ((bf16[8,2,8,8192]{3,2,1,0:T(8,128)(2,1)}), bf16[8,2,8,8192]{3,2,1,0:T(8,128)(2,1)}, u32[]{:S(2)}, u32[]{:S(2)}) async-start(bf16[8,2,8,8192]{3,2,1,0:T(8,128)(2,1)} %bitcast.69), calls=%async_computation | async-start | bytes 4194304 | tf_op jit(solution)/shard_map/all_to_all | solution.py:28
  107.6 87.9 %collective-permute-start.3 = (bf16[2,64,9216]{2,1,0:T(8,128)(2,1)}, bf16[2,64,9216]{2,1,0:T(8,128)(2,1)}, u32[]{:S(2)}, u32[]{:S(2)}) collective-permute-start(bf16[2,64,9216]{2,1,0:T(8,128)(2,1)} %collective-permute-done), channel_id=1, source_target_pairs={{4,8},{5,9},{6,10},{7,11},{8,4},{9,5},{10,6},{11,7},{20,24},{21,25... | collective-permute-start | bytes 7077896 | tf_op jit(solution)/shard_map/ppermute | solution.py:25
  111.2 105.6 %all-to-all-start.1 = ((bf16[8,6,8,8192]{3,2,1,0:T(8,128)(2,1)}), bf16[8,6,8,8192]{3,2,1,0:T(8,128)(2,1)}, u32[]{:S(2)}, u32[]{:S(2)}) async-start(bf16[8,6,8,8192]{3,2,1,0:T(8,128)(2,1)} %bitcast.70), calls=%async_computation.1 | async-start | bytes 12582912 | tf_op jit(solution)/shard_map/all_to_all | solution.py:28
  119.1 72.2 %collective-permute-start.4 = (bf16[8,2,8,8192]{3,2,0,1:T(8,128)(2,1)}, bf16[8,2,8,8192]{3,2,0,1:T(8,128)(2,1)}, u32[]{:S(2)}, u32[]{:S(2)}) collective-permute-start(bf16[8,2,8,8192]{3,2,0,1:T(8,128)(2,1)} %copy.16), channel_id=1, source_target_pairs={{0,4},{1,5},{2,6},{3,7},{12,8},{13,9},{14,10},{15,11},{16,20},{17,... | collective-permute-start | bytes 6291464 | tf_op jit(solution)/shard_map/ppermute | solution.py:25
  120.4 79.6 %collective-permute-start.2 = (bf16[2,64,9216]{2,1,0:T(8,128)(2,1)}, bf16[2,64,9216]{2,1,0:T(8,128)(2,1)}, u32[]{:S(2)}, u32[]{:S(2)}) collective-permute-start(bf16[2,64,9216]{2,1,0:T(8,128)(2,1)} %collective-permute-done.1), channel_id=1, source_target_pairs={{4,0},{5,1},{6,2},{7,3},{8,12},{9,13},{10,14},{11,15},{20,16},{21,... | collective-permute-start | bytes 7077896 | tf_op jit(solution)/shard_map/ppermute | solution.py:25
  198.6 18.2 %collective-permute-start.5 = (bf16[8,2,8,1024]{3,2,0,1:T(8,128)(2,1)S(1)}, bf16[8,2,8,1024]{3,2,0,1:T(8,128)(2,1)S(1)}, u32[]{:S(2)}, u32[]{:S(2)}) collective-permute-start(bf16[8,2,8,1024]{3,2,0,1:T(8,128)(2,1)S(1)} %fusion.11), channel_id=1, source_target_pairs={{4,0},{5,1},{6,2},{7,3},{8,12},{9,13},{10,14},{11,15},{20,16},{21,... | collective-permute-start | bytes 786440 | tf_op jit(solution)/shard_map/ppermute | solution.py:25
  224.5 20.5 %all-to-all-start.2 = ((bf16[8,8,8,1024]{3,2,1,0:T(8,128)(2,1)}), bf16[8,8,8,1024]{3,2,1,0:T(8,128)(2,1)S(1)}, u32[]{:S(2)}, u32[]{:S(2)}) async-start(bf16[8,8,8,1024]{3,2,1,0:T(8,128)(2,1)} %copy.18), calls=%async_computation.2 | async-start | bytes 2097152 | tf_op jit(solution)/shard_map/all_to_all | solution.py:28
  247.1 15.9 %copy-start.1 = (bf16[4,64,1024]{2,1,0:T(8,128)(2,1)S(1)}, bf16[4,64,1024]{2,1,0:T(8,128)(2,1)}, u32[]{:S(2)}) copy-start(bf16[4,64,1024]{2,1,0:T(8,128)(2,1)} %param.9) | copy-start | bytes 1572868
Sparse Core Ops, SparseCore 0:
  9.5 218.1 all-gather.1

commit v5 on v4

--- a/solution.py
+++ b/solution.py
@@ -97,14 +97,14 @@
 
         if relayed:
             edge = (here == 0) | (here == 3)
-            far_rows = exchange(outgoing(3, 1))
             near_sent = outgoing(0, 3)
+            far_rows = after(exchange(outgoing(3, 1)), near_sent)
             near_rows = exchange(near_sent)
-            pair = after(hop(own, (0, 1), (1, 0), (2, 3), (3, 2)), (far_rows, near_sent))
-            mid = after(hop(own, (1, 2), (2, 1)), (far_rows, near_sent))
+            extra_rows = hop(far_rows, (0, 1), (3, 2))
+            pair = after(hop(own, (0, 1), (1, 0), (2, 3), (3, 2)), extra_rows)
+            mid = after(hop(own, (1, 2), (2, 1)), extra_rows)
             crossed = hop(pair, (1, 2), (2, 1))
             outer = hop(mid, (1, 0), (2, 3))
-            extra_rows = hop(far_rows, (0, 1), (3, 2))
             base = jnp.dot(tokens, lax.all_gather(value_weight, "ad", axis=0, tiled=True), preferred_element_type=F32)
             extra = hop(adapt(extra_rows, crossed, model_width), (1, 0), (2, 3))
             far = jnp.where(edge, extra, adapt(far_rows, crossed, model_width))

time: 275 us -> 330 us (1.20); the launches traced: 270 us -> 330 us
  waiting for transfers between devices: 166 us -> 229 us
  starting transfers between devices: 32.3 us -> 27.7 us
    ppermute x6, waiting for transfers between devices: 130 us -> 191 us  [hop(): return lax.ppermute(array, 'ad', moves)]
  transfers between devices with their start and end apart: 10 -> 10, of which waited for: 6 -> 5; matrix products, arithmetic and copies ran while one was open for 15% -> 13% of each run, Pallas kernels for 0% -> 0%
where the time goes in v5:
time: 330 us
  waiting for transfers between devices  229 us (69%)
  matrix products  47 us (14%)
  starting transfers between devices  27.7 us (8%)
  between operations  13.5 us (4%)
  other arithmetic  7.08 us (2%)
  local copies, waits for them, and re-layouts  5.95 us (2%)
    ppermute x6, waiting for transfers between devices, hop(): return lax.ppermute(array, 'ad', moves)  191 us
    all_to_all x3, waiting for transfers between devices, exchange(): lax.all_to_all(array, ('rep', 'ad'), split_axis=0, concat_axis=0, tiled=T...  37.1 us
    dot_general x1, matrix products, on_device(): jnp.dot(tokens, lax.all_gather(value_weight, 'ad', axis=0, tiled=True), p...  15.9 us
    ppermute x6, starting transfers between devices, hop(): return lax.ppermute(array, 'ad', moves)  14.8 us
    dot_general x2, matrix products, outgoing(): sent = jnp.dot(pick, tokens, preferred_element_type=F32).astype(BF16)  14.8 us
    dot_general x3, matrix products, adapt(): jnp.einsum('sajr,arn->sajn', latent, panel[:, :, model_width:], preferred...  14.2 us
    all_to_all x3, starting transfers between devices, exchange(): lax.all_to_all(array, ('rep', 'ad'), split_axis=0, concat_axis=0, tiled=T...  12.8 us
  transfers between devices with their start and end apart: 10, of which 5 were waited for; matrix products, arithmetic and copies ran while one was open for 13% of the time, Pallas kernels for 0%

profile of v5, /device:TPU:8, one launch (start us, length us, event | category | flops | bytes accessed | tf_op | source)
XLA Modules:
  0.0 329.8 jit_solution(13903572570155228914)
XLA Ops:
  6.5 0.0 copy-start
  6.5 0.0 all-gather.2.cloned.1.call-start
  6.5 0.7 all-gather.2.cloned.1.call-update
  7.3 0.8 select_reduce_fusion
  8.1 0.3 convert_reduce_fusion
  8.4 6.0 %convolution_convert_fusion.1 = bf16[128,8192]{1,0:T(8,128)(2,1)} fusion(bf16[512,8192]{1,0:T(8,128)(2,1)} %param.6, s32[512]{0:T(512)S(1)} %fusion.60, s32[128]{0:T(128)S(1)} %fusion.93), kind=kOutput, calls=%fused_computation.1 | convolution fusion | flops 1074855936 | bytes 10488320 | tf_op jit(solution)/shard_map/dot_general | solution.py:88
  14.4 3.7 %all-to-all-start = ((bf16[8,2,8,8192]{3,2,1,0:T(8,128)(2,1)}), bf16[8,2,8,8192]{3,2,1,0:T(8,128)(2,1)S(1)}, u32[]{:S(2)}, u32[]{:S(2)}) async-start(bf16[8,2,8,8192]{3,2,1,0:T(8,128)(2,1)} %bitcast.69), calls=%async_computation | async-start | bytes 4194304 | tf_op jit(solution)/shard_map/all_to_all | solution.py:28
  18.1 0.0 copy-done
  18.1 2.1 dynamic-slice_bitcast_fusion
  20.2 0.0 copy-start.2
  20.2 1.3 copy-done.2
  21.5 1.6 pad_maximum_fusion.5
  23.1 0.4 collective-permute-start
  23.6 8.8 %convolution_convert_fusion = bf16[384,8192]{1,0:T(8,128)(2,1)} fusion(bf16[512,8192]{1,0:T(8,128)(2,1)} %param.6, s32[512]{0:T(512)S(1)} %fusion.60, s32[384]{0:T(512)S(1)} %fusion.69), kind=kOutput, calls=%fused_computation | convolution fusion | flops 3224567808 | bytes 14683648 | tf_op jit(solution)/shard_map/dot_general | solution.py:88
  32.3 22.7 %all-to-all-done = bf16[8,2,8,8192]{3,2,1,0:T(8,128)(2,1)S(1)} async-done(((bf16[8,2,8,8192]{3,2,1,0:T(8,128)(2,1)}), bf16[8,2,8,8192]{3,2,1,0:T(8,128)(2,1)S(1)}, u32[]{:S(2)}, u32[]{:S(2)}) %all-to-all-start) | async-done | bytes 2097184 | tf_op jit(solution)/shard_map/all_to_all | solution.py:28
  55.0 1.5 copy.15
  56.5 1.3 collective-permute-start.1
  57.8 3.5 %collective-permute-start.2 = (bf16[2,64,9216]{2,1,0:T(8,128)(2,1)}, bf16[2,64,9216]{2,1,0:T(8,128)(2,1)}, u32[]{:S(2)}, u32[]{:S(2)}) collective-permute-start(bf16[2,64,9216]{2,1,0:T(8,128)(2,1)} %pad_maximum_fusion.5), channel_id=1, source_target_pairs={{4,8},{5,9},{6,10},{7,11},{8,4},{9,5},{10,6},{11,7},{20,24},{21,25... | collective-permute-start | bytes 7077896 | tf_op jit(solution)/shard_map/ppermute | solution.py:25
  61.3 4.8 %all-to-all-start.1 = ((bf16[8,6,8,8192]{3,2,1,0:T(8,128)(2,1)}), bf16[8,6,8,8192]{3,2,1,0:T(8,128)(2,1)}, u32[]{:S(2)}, u32[]{:S(2)}) async-start(bf16[8,6,8,8192]{3,2,1,0:T(8,128)(2,1)} %bitcast.70), calls=%async_computation.1 | async-start | bytes 12582912 | tf_op jit(solution)/shard_map/all_to_all | solution.py:28
  66.0 65.2 %collective-permute-done = bf16[2,64,9216]{2,1,0:T(8,128)(2,1)} collective-permute-done((bf16[2,64,9216]{2,1,0:T(8,128)(2,1)}, bf16[2,64,9216]{2,1,0:T(8,128)(2,1)}, u32[]{:S(2)}, u32[]{:S(2)}) %collective-permute-start) | collective-permute-done | bytes 2359328 | tf_op jit(solution)/shard_map/ppermute | solution.py:25
  131.3 74.1 %collective-permute-done.1 = bf16[8,2,8,8192]{3,2,0,1:T(8,128)(2,1)} collective-permute-done((bf16[8,2,8,8192]{3,2,0,1:T(8,128)(2,1)}, bf16[8,2,8,8192]{3,2,0,1:T(8,128)(2,1)}, u32[]{:S(2)}, u32[]{:S(2)}) %collective-permute-start.1) | collective-permute-done | bytes 2097184 | tf_op jit(solution)/shard_map/ppermute | solution.py:25
  205.3 5.6 %collective-permute-start.4 = (bf16[2,64,9216]{2,1,0:T(8,128)(2,1)}, bf16[2,64,9216]{2,1,0:T(8,128)(2,1)}, u32[]{:S(2)}, u32[]{:S(2)}) collective-permute-start(bf16[2,64,9216]{2,1,0:T(8,128)(2,1)} %collective-permute-done), channel_id=1, source_target_pairs={{4,8},{5,9},{6,10},{7,11},{8,4},{9,5},{10,6},{11,7},{20,24},{21,25... | collective-permute-start | bytes 7077896 | tf_op jit(solution)/shard_map/ppermute | solution.py:25
  211.0 0.0 collective-permute-done.2
  211.0 2.7 collective-permute-start.3
  213.6 51.5 %collective-permute-done.4 = bf16[2,64,9216]{2,1,0:T(8,128)(2,1)} collective-permute-done((bf16[2,64,9216]{2,1,0:T(8,128)(2,1)}, bf16[2,64,9216]{2,1,0:T(8,128)(2,1)}, u32[]{:S(2)}, u32[]{:S(2)}) %collective-permute-start.4) | collective-permute-done | bytes 2359328 | tf_op jit(solution)/shard_map/ppermute | solution.py:25
  265.1 3.2 fusion.11
  268.3 1.3 collective-permute-start.5
  269.6 0.0 collective-permute-done.3
  269.6 3.3 %broadcast_select_fusion = bf16[2,64,9216]{2,1,0:T(8,128)(2,1)} fusion(bf16[2,64,9216]{2,1,0:T(8,128)(2,1)} %collective-permute-done.3, bf16[2,64,9216]{2,1,0:T(8,128)(2,1)} %collective-permute-done.2, pred[]{:T(512)S(6)} %or.3), kind=kLoop, calls=%fused_computation.10 | loop fusion | flops 1179648 | bytes 7077889 | tf_op jit(solution)/shard_map/jit(_where)/select_n | solution.py:111
  272.9 0.0 all-to-all-done.1
  272.9 7.7 %fusion.7 = bf16[8,6,8,1024]{3,2,0,1:T(8,128)(2,1)} fusion(bf16[8,6,8,8192]{3,2,1,0:T(8,128)(2,1)} %all-to-all-done.1, bf16[2,64,9216]{2,1,0:T(8,128)(2,1)} %broadcast_select_fusion, bf16[2,64,9216]{2,1,0:T(8,128)(2,1)} %collective-permute-done, bf16[2,64,1024]{2,1,0:T(8,128)(2,1)S(1)} %constant_dynamic-slice_fusion, bf16[2,64,8192]{2,1,0:T(8,128)(2,1)} %copy-done.2), kind=kOutput, calls=%fused_computation.17 | convolution fusion | flops 482107392 | bytes 14155776 | tf_op jit(solution)/shard_map/sajr,arn->sajn/dot_general | solution.py:37
  280.6 0.0 copy-start.3
  280.6 3.3 %fusion.10 = bf16[8,2,8,1024]{3,2,0,1:T(8,128)(2,1)} fusion(bf16[2,64,9216]{2,1,0:T(8,128)(2,1)} %collective-permute-done.4, bf16[8,2,8,8192]{3,2,1,0:T(8,128)(2,1)S(1)} %all-to-all-done), kind=kOutput, calls=%fused_computation.22 | convolution fusion | flops 151265280 | bytes 4718592 | tf_op jit(solution)/shard_map/sajr,arn->sajn/dot_general | solution.py:37
  284.0 0.0 collective-permute-done.5
  284.0 1.0 broadcast_select_fusion.1
  285.0 0.0 copy-done.3
  285.0 0.1 pad_maximum_fusion.6
  285.1 1.1 copy.18
  286.1 4.3 %all-to-all-start.2 = ((bf16[8,8,8,1024]{3,2,1,0:T(8,128)(2,1)}), bf16[8,8,8,1024]{3,2,1,0:T(8,128)(2,1)S(1)}, u32[]{:S(2)}, u32[]{:S(2)}) async-start(bf16[8,8,8,1024]{3,2,1,0:T(8,128)(2,1)} %copy.18), calls=%async_computation.2 | async-start | bytes 2097152 | tf_op jit(solution)/shard_map/all_to_all | solution.py:28
  290.5 14.5 %all-to-all-done.2 = bf16[8,8,8,1024]{3,2,1,0:T(8,128)(2,1)S(1)} async-done(((bf16[8,8,8,1024]{3,2,1,0:T(8,128)(2,1)}), bf16[8,8,8,1024]{3,2,1,0:T(8,128)(2,1)S(1)}, u32[]{:S(2)}, u32[]{:S(2)}) %all-to-all-start.2) | async-done | bytes 1048608 | tf_op jit(solution)/shard_map/all_to_all | solution.py:28
  304.9 2.1 fusion.31
  307.0 0.0 all-gather.2.cloned.1.call-done
  307.0 0.0 copy-start.1
  307.0 15.9 %add_convert_fusion = bf16[512,1024]{1,0:T(8,128)(2,1)} fusion(f32[512,1024]{1,0:T(8,128)} %fusion.31, bf16[512,8192]{1,0:T(8,128)(2,1)} %param.6, bf16[8192,1024]{1,0:T(8,128)(2,1)} %all-gather.2.cloned.1.call-done), kind=kOutput, calls=%fused_computation.12 | convolution fusion | flops 8590983168 | bytes 28311552 | tf_op jit(solution)/shard_map/dot_general | solution.py:108
  322.9 0.0 copy-done.1
  (5 shorter events, 0.1 us)
Async XLA Ops:
  6.5 11.6 %copy-start = (bf16[4,64,1024]{2,1,0:T(8,128)(2,1)S(1)}, bf16[4,64,1024]{2,1,0:T(8,128)(2,1)}, u32[]{:S(2)}) copy-start(bf16[4,64,1024]{2,1,0:T(8,128)(2,1)} %param.9) | copy-start | bytes 1572868
  6.5 300.5 %all-gather.2.cloned.1.call-start = ((), (), s32[]{:S(2)}) async-start(), calls=%async_computation.3 | async-start | bytes 17825792 | tf_op jit(solution)/shard_map/all_gather | solution.py:108
  14.4 40.6 %all-to-all-start = ((bf16[8,2,8,8192]{3,2,1,0:T(8,128)(2,1)}), bf16[8,2,8,8192]{3,2,1,0:T(8,128)(2,1)S(1)}, u32[]{:S(2)}, u32[]{:S(2)}) async-start(bf16[8,2,8,8192]{3,2,1,0:T(8,128)(2,1)} %bitcast.69), calls=%async_computation | async-start | bytes 4194304 | tf_op jit(solution)/shard_map/all_to_all | solution.py:28
  20.2 1.3 copy-start.2
  23.1 108.1 %collective-permute-start = (bf16[2,64,9216]{2,1,0:T(8,128)(2,1)}, bf16[2,64,9216]{2,1,0:T(8,128)(2,1)}, u32[]{:S(2)}, u32[]{:S(2)}) collective-permute-start(bf16[2,64,9216]{2,1,0:T(8,128)(2,1)} %pad_maximum_fusion.5), channel_id=1, source_target_pairs={{0,4},{1,5},{2,6},{3,7},{4,0},{5,1},{6,2},{7,3},{8,12},{9,13},{10,... | collective-permute-start | bytes 7077896 | tf_op jit(solution)/shard_map/ppermute | solution.py:25
  56.5 148.8 %collective-permute-start.1 = (bf16[8,2,8,8192]{3,2,0,1:T(8,128)(2,1)}, bf16[8,2,8,8192]{3,2,0,1:T(8,128)(2,1)}, u32[]{:S(2)}, u32[]{:S(2)}) collective-permute-start(bf16[8,2,8,8192]{3,2,0,1:T(8,128)(2,1)} %copy.15), channel_id=1, source_target_pairs={{0,4},{1,5},{2,6},{3,7},{12,8},{13,9},{14,10},{15,11},{16,20},{17,... | collective-permute-start | bytes 6291464 | tf_op jit(solution)/shard_map/ppermute | solution.py:25
  57.8 153.2 %collective-permute-start.2 = (bf16[2,64,9216]{2,1,0:T(8,128)(2,1)}, bf16[2,64,9216]{2,1,0:T(8,128)(2,1)}, u32[]{:S(2)}, u32[]{:S(2)}) collective-permute-start(bf16[2,64,9216]{2,1,0:T(8,128)(2,1)} %pad_maximum_fusion.5), channel_id=1, source_target_pairs={{4,8},{5,9},{6,10},{7,11},{8,4},{9,5},{10,6},{11,7},{20,24},{21,25... | collective-permute-start | bytes 7077896 | tf_op jit(solution)/shard_map/ppermute | solution.py:25
  61.3 211.7 %all-to-all-start.1 = ((bf16[8,6,8,8192]{3,2,1,0:T(8,128)(2,1)}), bf16[8,6,8,8192]{3,2,1,0:T(8,128)(2,1)}, u32[]{:S(2)}, u32[]{:S(2)}) async-start(bf16[8,6,8,8192]{3,2,1,0:T(8,128)(2,1)} %bitcast.70), calls=%async_computation.1 | async-start | bytes 12582912 | tf_op jit(solution)/shard_map/all_to_all | solution.py:28
  205.3 59.8 %collective-permute-start.4 = (bf16[2,64,9216]{2,1,0:T(8,128)(2,1)}, bf16[2,64,9216]{2,1,0:T(8,128)(2,1)}, u32[]{:S(2)}, u32[]{:S(2)}) collective-permute-start(bf16[2,64,9216]{2,1,0:T(8,128)(2,1)} %collective-permute-done), channel_id=1, source_target_pairs={{4,8},{5,9},{6,10},{7,11},{8,4},{9,5},{10,6},{11,7},{20,24},{21,25... | collective-permute-start | bytes 7077896 | tf_op jit(solution)/shard_map/ppermute | solution.py:25
  211.0 58.6 %collective-permute-start.3 = (bf16[2,64,9216]{2,1,0:T(8,128)(2,1)}, bf16[2,64,9216]{2,1,0:T(8,128)(2,1)}, u32[]{:S(2)}, u32[]{:S(2)}) collective-permute-start(bf16[2,64,9216]{2,1,0:T(8,128)(2,1)} %collective-permute-done.2), channel_id=1, source_target_pairs={{4,0},{5,1},{6,2},{7,3},{8,12},{9,13},{10,14},{11,15},{20,16},{21,... | collective-permute-start | bytes 7077896 | tf_op jit(solution)/shard_map/ppermute | solution.py:25
  268.3 15.7 %collective-permute-start.5 = (bf16[8,2,8,1024]{3,2,0,1:T(8,128)(2,1)S(1)}, bf16[8,2,8,1024]{3,2,0,1:T(8,128)(2,1)S(1)}, u32[]{:S(2)}, u32[]{:S(2)}) collective-permute-start(bf16[8,2,8,1024]{3,2,0,1:T(8,128)(2,1)S(1)} %fusion.11), channel_id=1, source_target_pairs={{4,0},{5,1},{6,2},{7,3},{8,12},{9,13},{10,14},{11,15},{20,16},{21,... | collective-permute-start | bytes 786440 | tf_op jit(solution)/shard_map/ppermute | solution.py:25
  280.6 4.3 %copy-start.3 = (bf16[8,6,8,1024]{3,2,0,1:T(8,128)(2,1)S(1)}, bf16[8,6,8,1024]{3,2,0,1:T(8,128)(2,1)}, u32[]{:S(2)}) copy-start(bf16[8,6,8,1024]{3,2,0,1:T(8,128)(2,1)} %fusion.7) | copy-start | bytes 2359300
  286.1 18.8 %all-to-all-start.2 = ((bf16[8,8,8,1024]{3,2,1,0:T(8,128)(2,1)}), bf16[8,8,8,1024]{3,2,1,0:T(8,128)(2,1)S(1)}, u32[]{:S(2)}, u32[]{:S(2)}) async-start(bf16[8,8,8,1024]{3,2,1,0:T(8,128)(2,1)} %copy.18), calls=%async_computation.2 | async-start | bytes 2097152 | tf_op jit(solution)/shard_map/all_to_all | solution.py:28
  307.0 15.9 %copy-start.1 = (bf16[4,64,1024]{2,1,0:T(8,128)(2,1)S(1)}, bf16[4,64,1024]{2,1,0:T(8,128)(2,1)}, u32[]{:S(2)}) copy-start(bf16[4,64,1024]{2,1,0:T(8,128)(2,1)} %param.9) | copy-start | bytes 1572868
Sparse Core Ops, SparseCore 0:
  9.5 210.7 all-gather.1

commit v6 on v4

--- a/solution.py
+++ b/solution.py
@@ -107,9 +107,10 @@
             extra_rows = hop(far_rows, (0, 1), (3, 2))
             base = jnp.dot(tokens, lax.all_gather(value_weight, "ad", axis=0, tiled=True), preferred_element_type=F32)
             extra = hop(adapt(extra_rows, crossed, model_width), (1, 0), (2, 3))
-            far = jnp.where(edge, extra, adapt(far_rows, crossed, model_width))
             panels = jnp.concatenate([own, pair, jnp.where(edge, outer, mid)], axis=0)
             near = adapt(near_rows, panels, model_width)
+            local = adapt(far_rows, crossed, model_width)
+            far = jnp.where(edge, after(extra, (near, local)), local)
             back = exchange(joined([near, far]))
         else:
             sent = outgoing(0, layers)
@@ -117,7 +118,7 @@
             panels = lax.all_gather(own, "ad", axis=0, tiled=True, axis_index_groups=columns)
             base = jnp.dot(tokens, lax.all_gather(value_weight, "ad", axis=0, tiled=True), preferred_element_type=F32)
             back = exchange(adapt(incoming, panels, model_width))
-        return (base + delta(back, 0, layers)).astype(BF16)
+        return (base + delta(after(back, base), 0, layers)).astype(BF16)
 
     in_specs = (
         P(("rep", "ad"), None),

time: 275 us -> 277 us (level); the launches traced: 270 us -> 276 us
  waiting for transfers between devices: 166 us -> 175 us
  starting transfers between devices: 32.3 us -> 25.9 us
    ppermute x6, waiting for transfers between devices: 130 us -> 155 us  [hop(): return lax.ppermute(array, 'ad', moves)]
    all_to_all x3, waiting for transfers between devices: 35.7 us -> 19.9 us  [exchange(): lax.all_to_all(array, ('rep', 'ad'), split_axis=0, concat_axis=0, tiled=T...]
    ppermute x6, starting transfers between devices: 17.1 us -> 13 us  [hop(): return lax.ppermute(array, 'ad', moves)]
  transfers between devices with their start and end apart: 10 -> 10, of which waited for: 6 -> 5; matrix products, arithmetic and copies ran while one was open for 15% -> 21% of each run, Pallas kernels for 0% -> 0%
where the time goes in v6:
time: 277 us; the launch traced here: 276 us
  waiting for transfers between devices  175 us (63%)
  matrix products  48 us (17%)
  starting transfers between devices  25.9 us (9%)
  between operations  13.5 us (5%)
  other arithmetic  6.41 us (2%)
  local copies, waits for them, and re-layouts  6.34 us (2%)
    ppermute x6, waiting for transfers between devices, hop(): return lax.ppermute(array, 'ad', moves)  155 us
    all_to_all x3, waiting for transfers between devices, exchange(): lax.all_to_all(array, ('rep', 'ad'), split_axis=0, concat_axis=0, tiled=T...  19.9 us
    dot_general x1, matrix products, on_device(): jnp.dot(tokens, lax.all_gather(value_weight, 'ad', axis=0, tiled=True), p...  15.8 us
    dot_general x2, matrix products, outgoing(): sent = jnp.dot(pick, tokens, preferred_element_type=F32).astype(BF16)  14.8 us
    dot_general x3, matrix products, adapt(): jnp.einsum('sajr,arn->sajn', latent, panel[:, :, model_width:], preferred...  14 us
    ppermute x6, starting transfers between devices, hop(): return lax.ppermute(array, 'ad', moves)  13 us
    all_to_all x3, starting transfers between devices, exchange(): lax.all_to_all(array, ('rep', 'ad'), split_axis=0, concat_axis=0, tiled=T...  12.9 us
  transfers between devices with their start and end apart: 10, of which 5 were waited for; matrix products, arithmetic and copies ran while one was open for 21% of the time, Pallas kernels for 0%

profile of v6, /device:TPU:8, one launch (start us, length us, event | category | flops | bytes accessed | tf_op | source)
XLA Modules:
  0.0 275.6 jit_solution(17640471348940346184)
XLA Ops:
  6.5 0.0 copy-start
  6.5 0.0 all-gather.2.cloned.1.call-start
  6.5 0.7 all-gather.2.cloned.1.call-update
  7.3 0.3 copy-done
  7.6 1.8 dynamic-slice_bitcast_fusion
  9.4 0.0 copy-start.2
  9.4 0.0 copy-start.3
  9.4 1.6 pad_maximum_fusion.5
  11.0 0.0 collective-permute-start
  11.0 0.0 copy-done.2
  11.0 0.0 copy-done.3
  11.0 0.1 select_reduce_fusion
  11.1 0.3 convert_reduce_fusion
  11.4 6.0 %convolution_convert_fusion.1 = bf16[128,8192]{1,0:T(8,128)(2,1)} fusion(bf16[512,8192]{1,0:T(8,128)(2,1)} %param.6, s32[512]{0:T(512)S(1)} %get-tuple-element.13, s32[128]{0:T(128)S(1)} %fusion.92), kind=kOutput, calls=%fused_computation.1 | convolution fusion | flops 1074855936 | bytes 10488320 | tf_op jit(solution)/shard_map/dot_general | solution.py:88
  17.4 4.4 %all-to-all-start = ((bf16[8,2,8,8192]{3,2,1,0:T(8,128)(2,1)}), bf16[8,2,8,8192]{3,2,1,0:T(8,128)(2,1)}, u32[]{:S(2)}, u32[]{:S(2)}) async-start(bf16[8,2,8,8192]{3,2,1,0:T(8,128)(2,1)} %bitcast.69), calls=%async_computation | async-start | bytes 4194304 | tf_op jit(solution)/shard_map/all_to_all | solution.py:28
  21.8 5.1 %collective-permute-start.1 = (bf16[2,64,9216]{2,1,0:T(8,128)(2,1)}, bf16[2,64,9216]{2,1,0:T(8,128)(2,1)}, u32[]{:S(2)}, u32[]{:S(2)}) collective-permute-start(bf16[2,64,9216]{2,1,0:T(8,128)(2,1)} %pad_maximum_fusion.5), channel_id=1, source_target_pairs={{4,8},{5,9},{6,10},{7,11},{8,4},{9,5},{10,6},{11,7},{20,24},{21,25... | collective-permute-start | bytes 7077896 | tf_op jit(solution)/shard_map/ppermute | solution.py:25
  26.9 8.8 %convolution_convert_fusion = bf16[384,8192]{1,0:T(8,128)(2,1)} fusion(bf16[512,8192]{1,0:T(8,128)(2,1)} %param.6, s32[512]{0:T(512)S(1)} %get-tuple-element.13, s32[384]{0:T(512)S(1)} %fusion.68), kind=kOutput, calls=%fused_computation | convolution fusion | flops 3224567808 | bytes 14683648 | tf_op jit(solution)/shard_map/dot_general | solution.py:88
  35.7 19.9 %all-to-all-done = bf16[8,2,8,8192]{3,2,1,0:T(8,128)(2,1)} async-done(((bf16[8,2,8,8192]{3,2,1,0:T(8,128)(2,1)}), bf16[8,2,8,8192]{3,2,1,0:T(8,128)(2,1)}, u32[]{:S(2)}, u32[]{:S(2)}) %all-to-all-start) | async-done | bytes 2097184 | tf_op jit(solution)/shard_map/all_to_all | solution.py:28
  55.6 4.8 %all-to-all-start.1 = ((bf16[8,6,8,8192]{3,2,1,0:T(8,128)(2,1)}), bf16[8,6,8,8192]{3,2,1,0:T(8,128)(2,1)}, u32[]{:S(2)}, u32[]{:S(2)}) async-start(bf16[8,6,8,8192]{3,2,1,0:T(8,128)(2,1)} %bitcast.70), calls=%async_computation.1 | async-start | bytes 12582912 | tf_op jit(solution)/shard_map/all_to_all | solution.py:28
  60.4 40.0 %collective-permute-done = bf16[2,64,9216]{2,1,0:T(8,128)(2,1)} collective-permute-done((bf16[2,64,9216]{2,1,0:T(8,128)(2,1)}, bf16[2,64,9216]{2,1,0:T(8,128)(2,1)}, u32[]{:S(2)}, u32[]{:S(2)}) %collective-permute-start) | collective-permute-done | bytes 2359328 | tf_op jit(solution)/shard_map/ppermute | solution.py:25
  100.4 2.7 collective-permute-start.3
  103.1 3.1 %copy.16 = bf16[8,2,8,8192]{3,2,0,1:T(8,128)(2,1)} copy(bf16[8,2,8,8192]{3,2,1,0:T(8,128)(2,1)} %all-to-all-done) | data formatting | bytes 4194304 | tf_op jit(solution)/shard_map/all_to_all | solution.py:28
  106.3 1.3 collective-permute-start.4
  107.6 19.7 %collective-permute-done.1 = bf16[2,64,9216]{2,1,0:T(8,128)(2,1)} collective-permute-done((bf16[2,64,9216]{2,1,0:T(8,128)(2,1)}, bf16[2,64,9216]{2,1,0:T(8,128)(2,1)}, u32[]{:S(2)}, u32[]{:S(2)}) %collective-permute-start.1) | collective-permute-done | bytes 2359328 | tf_op jit(solution)/shard_map/ppermute | solution.py:25
  127.2 2.7 collective-permute-start.2
  129.9 69.2 %collective-permute-done.4 = bf16[8,2,8,8192]{3,2,0,1:T(8,128)(2,1)} collective-permute-done((bf16[8,2,8,8192]{3,2,0,1:T(8,128)(2,1)}, bf16[8,2,8,8192]{3,2,0,1:T(8,128)(2,1)}, u32[]{:S(2)}, u32[]{:S(2)}) %collective-permute-start.4) | collective-permute-done | bytes 2097184 | tf_op jit(solution)/shard_map/ppermute | solution.py:25
  199.0 25.9 %collective-permute-done.3 = bf16[2,64,9216]{2,1,0:T(8,128)(2,1)} collective-permute-done((bf16[2,64,9216]{2,1,0:T(8,128)(2,1)}, bf16[2,64,9216]{2,1,0:T(8,128)(2,1)}, u32[]{:S(2)}, u32[]{:S(2)}) %collective-permute-start.3) | collective-permute-done | bytes 2359328 | tf_op jit(solution)/shard_map/ppermute | solution.py:25
  225.0 3.9 %fusion.11 = bf16[8,2,8,1024]{3,2,0,1:T(8,128)(2,1)} fusion(bf16[8,2,8,8192]{3,2,0,1:T(8,128)(2,1)} %collective-permute-done.4, bf16[2,64,9216]{2,1,0:T(8,128)(2,1)} %collective-permute-done.3), kind=kOutput, calls=%fused_computation.23 | convolution fusion | flops 151265280 | bytes 4718592 | tf_op jit(solution)/shard_map/sajr,arn->sajn/dot_general | solution.py:37
  228.9 1.3 collective-permute-start.5
  230.2 3.9 %fusion.10 = bf16[8,2,8,1024]{3,2,0,1:T(8,128)(2,1)} fusion(bf16[2,64,9216]{2,1,0:T(8,128)(2,1)} %collective-permute-done.3, bf16[8,2,8,8192]{3,2,1,0:T(8,128)(2,1)} %all-to-all-done), kind=kOutput, calls=%fused_computation.22 | convolution fusion | flops 151265280 | bytes 4718592 | tf_op jit(solution)/shard_map/sajr,arn->sajn/dot_general | solution.py:37
  234.1 0.0 collective-permute-done.2
  234.1 3.4 %broadcast_select_fusion = bf16[2,64,9216]{2,1,0:T(8,128)(2,1)} fusion(bf16[2,64,9216]{2,1,0:T(8,128)(2,1)} %collective-permute-done.2, bf16[2,64,9216]{2,1,0:T(8,128)(2,1)} %collective-permute-done.1, pred[]{:T(512)S(6)} %or.3), kind=kLoop, calls=%fused_computation.10 | loop fusion | flops 1179648 | bytes 7077889 | tf_op jit(solution)/shard_map/jit(_where)/select_n | solution.py:110
  237.4 0.0 all-to-all-done.1
  237.4 6.2 %fusion.7 = bf16[8,6,8,1024]{3,2,0,1:T(8,128)(2,1)S(1)} fusion(bf16[8,6,8,8192]{3,2,1,0:T(8,128)(2,1)} %all-to-all-done.1, bf16[2,64,9216]{2,1,0:T(8,128)(2,1)} %broadcast_select_fusion, bf16[2,64,9216]{2,1,0:T(8,128)(2,1)} %collective-permute-done, bf16[2,64,1024]{2,1,0:T(8,128)(2,1)S(1)} %constant_dynamic-slice_fusion, ...), kind=kOutput, calls=%fused_computation.17 | convolution fusion | flops 482107392 | bytes 14155776 | tf_op jit(solution)/shard_map/sajr,arn->sajn/dot_general | solution.py:37
  243.6 0.0 collective-permute-done.5
  243.7 1.0 broadcast_select_fusion.1
  244.6 0.1 pad_maximum_fusion.6
  244.7 1.1 copy.18
  245.8 3.7 %all-to-all-start.2 = ((bf16[8,8,8,1024]{3,2,1,0:T(8,128)(2,1)}), bf16[8,8,8,1024]{3,2,1,0:T(8,128)(2,1)S(1)}, u32[]{:S(2)}, u32[]{:S(2)}) async-start(bf16[8,8,8,1024]{3,2,1,0:T(8,128)(2,1)} %copy.18), calls=%async_computation.2 | async-start | bytes 2097152 | tf_op jit(solution)/shard_map/all_to_all | solution.py:28
  249.6 0.0 all-gather.2.cloned.1.call-done
  249.6 0.0 copy-start.1
  249.6 15.8 %fusion.99 = f32[512,1024]{1,0:T(8,128)} fusion(bf16[512,8192]{1,0:T(8,128)(2,1)} %param.6, bf16[8192,1024]{1,0:T(8,128)(2,1)} %all-gather.2.cloned.1.call-done), kind=kOutput, calls=%fused_computation.144 | convolution fusion | flops 8589934592 | bytes 27262976 | tf_op jit(solution)/shard_map/dot_general | solution.py:108
  265.4 0.0 all-to-all-done.2
  265.4 3.3 %add_convert_fusion = bf16[512,1024]{1,0:T(8,128)(2,1)} fusion(f32[512,1024]{1,0:T(8,128)} %fusion.99, bf16[512,1024]{1,0:T(8,128)(2,1)S(1)} %bitcast.71, s32[512]{0:T(512)S(1)} %get-tuple-element.14, s32[512]{0:T(512)S(1)} %get-tuple-element.13), kind=kOutput, calls=%fused_computation.12 | convolution fusion | flops 538181632 | bytes 4198400 | tf_op jit(solution)/shard_map/dot_general | solution.py:93
  268.7 0.0 copy-done.1
  (4 shorter events, 0.1 us)
Async XLA Ops:
  6.5 1.0 copy-start
  6.5 243.0 %all-gather.2.cloned.1.call-start = ((), (), s32[]{:S(2)}) async-start(), calls=%async_computation.3 | async-start | bytes 17825792 | tf_op jit(solution)/shard_map/all_gather | solution.py:108
  9.4 1.6 copy-start.2
  9.4 1.6 copy-start.3
  11.0 89.4 %collective-permute-start = (bf16[2,64,9216]{2,1,0:T(8,128)(2,1)}, bf16[2,64,9216]{2,1,0:T(8,128)(2,1)}, u32[]{:S(2)}, u32[]{:S(2)}) collective-permute-start(bf16[2,64,9216]{2,1,0:T(8,128)(2,1)} %pad_maximum_fusion.5), channel_id=1, source_target_pairs={{0,4},{1,5},{2,6},{3,7},{4,0},{5,1},{6,2},{7,3},{8,12},{9,13},{10,... | collective-permute-start | bytes 7077896 | tf_op jit(solution)/shard_map/ppermute | solution.py:25
  17.4 38.2 %all-to-all-start = ((bf16[8,2,8,8192]{3,2,1,0:T(8,128)(2,1)}), bf16[8,2,8,8192]{3,2,1,0:T(8,128)(2,1)}, u32[]{:S(2)}, u32[]{:S(2)}) async-start(bf16[8,2,8,8192]{3,2,1,0:T(8,128)(2,1)} %bitcast.69), calls=%async_computation | async-start | bytes 4194304 | tf_op jit(solution)/shard_map/all_to_all | solution.py:28
  21.8 105.4 %collective-permute-start.1 = (bf16[2,64,9216]{2,1,0:T(8,128)(2,1)}, bf16[2,64,9216]{2,1,0:T(8,128)(2,1)}, u32[]{:S(2)}, u32[]{:S(2)}) collective-permute-start(bf16[2,64,9216]{2,1,0:T(8,128)(2,1)} %pad_maximum_fusion.5), channel_id=1, source_target_pairs={{4,8},{5,9},{6,10},{7,11},{8,4},{9,5},{10,6},{11,7},{20,24},{21,25... | collective-permute-start | bytes 7077896 | tf_op jit(solution)/shard_map/ppermute | solution.py:25
  55.6 181.8 %all-to-all-start.1 = ((bf16[8,6,8,8192]{3,2,1,0:T(8,128)(2,1)}), bf16[8,6,8,8192]{3,2,1,0:T(8,128)(2,1)}, u32[]{:S(2)}, u32[]{:S(2)}) async-start(bf16[8,6,8,8192]{3,2,1,0:T(8,128)(2,1)} %bitcast.70), calls=%async_computation.1 | async-start | bytes 12582912 | tf_op jit(solution)/shard_map/all_to_all | solution.py:28
  100.4 124.6 %collective-permute-start.3 = (bf16[2,64,9216]{2,1,0:T(8,128)(2,1)}, bf16[2,64,9216]{2,1,0:T(8,128)(2,1)}, u32[]{:S(2)}, u32[]{:S(2)}) collective-permute-start(bf16[2,64,9216]{2,1,0:T(8,128)(2,1)} %collective-permute-done), channel_id=1, source_target_pairs={{4,8},{5,9},{6,10},{7,11},{8,4},{9,5},{10,6},{11,7},{20,24},{21,25... | collective-permute-start | bytes 7077896 | tf_op jit(solution)/shard_map/ppermute | solution.py:25
  106.3 92.8 %collective-permute-start.4 = (bf16[8,2,8,8192]{3,2,0,1:T(8,128)(2,1)}, bf16[8,2,8,8192]{3,2,0,1:T(8,128)(2,1)}, u32[]{:S(2)}, u32[]{:S(2)}) collective-permute-start(bf16[8,2,8,8192]{3,2,0,1:T(8,128)(2,1)} %copy.16), channel_id=1, source_target_pairs={{0,4},{1,5},{2,6},{3,7},{12,8},{13,9},{14,10},{15,11},{16,20},{17,... | collective-permute-start | bytes 6291464 | tf_op jit(solution)/shard_map/ppermute | solution.py:25
  127.2 106.9 %collective-permute-start.2 = (bf16[2,64,9216]{2,1,0:T(8,128)(2,1)}, bf16[2,64,9216]{2,1,0:T(8,128)(2,1)}, u32[]{:S(2)}, u32[]{:S(2)}) collective-permute-start(bf16[2,64,9216]{2,1,0:T(8,128)(2,1)} %collective-permute-done.1), channel_id=1, source_target_pairs={{4,0},{5,1},{6,2},{7,3},{8,12},{9,13},{10,14},{11,15},{20,16},{21,... | collective-permute-start | bytes 7077896 | tf_op jit(solution)/shard_map/ppermute | solution.py:25
  228.9 14.8 %collective-permute-start.5 = (bf16[8,2,8,1024]{3,2,0,1:T(8,128)(2,1)}, bf16[8,2,8,1024]{3,2,0,1:T(8,128)(2,1)S(1)}, u32[]{:S(2)}, u32[]{:S(2)}) collective-permute-start(bf16[8,2,8,1024]{3,2,0,1:T(8,128)(2,1)} %fusion.11), channel_id=1, source_target_pairs={{4,0},{5,1},{6,2},{7,3},{8,12},{9,13},{10,14},{11,15},{20,16},{21,... | collective-permute-start | bytes 786440 | tf_op jit(solution)/shard_map/ppermute | solution.py:25
  245.8 19.6 %all-to-all-start.2 = ((bf16[8,8,8,1024]{3,2,1,0:T(8,128)(2,1)}), bf16[8,8,8,1024]{3,2,1,0:T(8,128)(2,1)S(1)}, u32[]{:S(2)}, u32[]{:S(2)}) async-start(bf16[8,8,8,1024]{3,2,1,0:T(8,128)(2,1)} %copy.18), calls=%async_computation.2 | async-start | bytes 2097152 | tf_op jit(solution)/shard_map/all_to_all | solution.py:28
  249.6 19.1 %copy-start.1 = (bf16[4,64,1024]{2,1,0:T(8,128)(2,1)S(1)}, bf16[4,64,1024]{2,1,0:T(8,128)(2,1)}, u32[]{:S(2)}) copy-start(bf16[4,64,1024]{2,1,0:T(8,128)(2,1)} %param.9) | copy-start | bytes 1572868
Sparse Core Ops, SparseCore 0:
  9.5 203.2 all-gather.1

commit v7 on v4

--- a/solution.py
+++ b/solution.py
@@ -117,7 +117,7 @@
             panels = lax.all_gather(own, "ad", axis=0, tiled=True, axis_index_groups=columns)
             base = jnp.dot(tokens, lax.all_gather(value_weight, "ad", axis=0, tiled=True), preferred_element_type=F32)
             back = exchange(adapt(incoming, panels, model_width))
-        return (base + delta(back, 0, layers)).astype(BF16)
+        return (base + delta(after(back, base), 0, layers)).astype(BF16)
 
     in_specs = (
         P(("rep", "ad"), None),

time: 275 us -> 262 us (0.953)
  waiting for transfers between devices: 166 us -> 152 us
    all_to_all x3, waiting for transfers between devices: 35.7 us -> 21.2 us  [exchange(): lax.all_to_all(array, ('rep', 'ad'), split_axis=0, concat_axis=0, tiled=T...]
  transfers between devices with their start and end apart: 10 -> 10, of which waited for: 6 -> 5; matrix products, arithmetic and copies ran while one was open for 15% -> 22% of each run, Pallas kernels for 0% -> 0%
where the time goes in v7:
time: 262 us; the launch traced here: 257 us
  waiting for transfers between devices  152 us (58%)
  matrix products  46.9 us (18%)
  starting transfers between devices  32.1 us (12%)
  between operations  13.6 us (5%)
  local copies, waits for them, and re-layouts  6.24 us (2%)
  other arithmetic  5.79 us (2%)
    ppermute x6, waiting for transfers between devices, hop(): return lax.ppermute(array, 'ad', moves)  130 us
    all_to_all x3, waiting for transfers between devices, exchange(): lax.all_to_all(array, ('rep', 'ad'), split_axis=0, concat_axis=0, tiled=T...  21.2 us
    ppermute x6, starting transfers between devices, hop(): return lax.ppermute(array, 'ad', moves)  17.1 us
    dot_general x1, matrix products, on_device(): jnp.dot(tokens, lax.all_gather(value_weight, 'ad', axis=0, tiled=True), p...  15.8 us
    all_to_all x3, starting transfers between devices, exchange(): lax.all_to_all(array, ('rep', 'ad'), split_axis=0, concat_axis=0, tiled=T...  15 us
    dot_general x2, matrix products, outgoing(): sent = jnp.dot(pick, tokens, preferred_element_type=F32).astype(BF16)  15 us
    dot_general x3, matrix products, adapt(): jnp.einsum('sajr,arn->sajn', latent, panel[:, :, model_width:], preferred...  12.8 us
  transfers between devices with their start and end apart: 10, of which 5 were waited for; matrix products, arithmetic and copies ran while one was open for 22% of the time, Pallas kernels for 0%

profile of v7, /device:TPU:8, one launch (start us, length us, event | category | flops | bytes accessed | tf_op | source)
XLA Modules:
  0.0 256.5 jit_solution(1343888431411949740)
XLA Ops:
  6.5 0.0 copy-start
  6.5 0.0 all-gather.2.cloned.1.call-start
  6.5 0.7 all-gather.2.cloned.1.call-update
  7.3 0.3 copy-done
  7.6 1.8 dynamic-slice_bitcast_fusion
  9.4 0.0 copy-start.2
  9.4 0.0 copy-start.3
  9.4 1.6 pad_maximum_fusion.5
  11.0 3.5 %collective-permute-start.1 = (bf16[2,64,9216]{2,1,0:T(8,128)(2,1)}, bf16[2,64,9216]{2,1,0:T(8,128)(2,1)}, u32[]{:S(2)}, u32[]{:S(2)}) collective-permute-start(bf16[2,64,9216]{2,1,0:T(8,128)(2,1)} %pad_maximum_fusion.5), channel_id=1, source_target_pairs={{4,8},{5,9},{6,10},{7,11},{8,4},{9,5},{10,6},{11,7},{20,24},{21,25... | collective-permute-start | bytes 7077896 | tf_op jit(solution)/shard_map/ppermute | solution.py:25
  14.5 0.1 collective-permute-start
  14.6 0.0 copy-done.2
  14.6 0.0 copy-done.3
  14.6 0.1 select_reduce_fusion
  14.7 0.3 convert_reduce_fusion
  15.0 6.1 %convolution_convert_fusion.1 = bf16[128,8192]{1,0:T(8,128)(2,1)} fusion(bf16[512,8192]{1,0:T(8,128)(2,1)} %param.6, s32[512]{0:T(512)S(1)} %get-tuple-element.11, s32[128]{0:T(128)S(1)} %fusion.92), kind=kOutput, calls=%fused_computation.1 | convolution fusion | flops 1074855936 | bytes 10488320 | tf_op jit(solution)/shard_map/dot_general | solution.py:88
  21.2 4.3 %all-to-all-start = ((bf16[8,2,8,8192]{3,2,1,0:T(8,128)(2,1)}), bf16[8,2,8,8192]{3,2,1,0:T(8,128)(2,1)}, u32[]{:S(2)}, u32[]{:S(2)}) async-start(bf16[8,2,8,8192]{3,2,1,0:T(8,128)(2,1)} %bitcast.69), calls=%async_computation | async-start | bytes 4194304 | tf_op jit(solution)/shard_map/all_to_all | solution.py:28
  25.5 8.8 %convolution_convert_fusion = bf16[384,8192]{1,0:T(8,128)(2,1)} fusion(bf16[512,8192]{1,0:T(8,128)(2,1)} %param.6, s32[512]{0:T(512)S(1)} %get-tuple-element.11, s32[384]{0:T(512)S(1)} %fusion.68), kind=kOutput, calls=%fused_computation | convolution fusion | flops 3224567808 | bytes 14683648 | tf_op jit(solution)/shard_map/dot_general | solution.py:88
  34.4 21.2 %all-to-all-done = bf16[8,2,8,8192]{3,2,1,0:T(8,128)(2,1)} async-done(((bf16[8,2,8,8192]{3,2,1,0:T(8,128)(2,1)}), bf16[8,2,8,8192]{3,2,1,0:T(8,128)(2,1)}, u32[]{:S(2)}, u32[]{:S(2)}) %all-to-all-start) | async-done | bytes 2097184 | tf_op jit(solution)/shard_map/all_to_all | solution.py:28
  55.6 52.0 %collective-permute-done = bf16[2,64,9216]{2,1,0:T(8,128)(2,1)} collective-permute-done((bf16[2,64,9216]{2,1,0:T(8,128)(2,1)}, bf16[2,64,9216]{2,1,0:T(8,128)(2,1)}, u32[]{:S(2)}, u32[]{:S(2)}) %collective-permute-start) | collective-permute-done | bytes 2359328 | tf_op jit(solution)/shard_map/ppermute | solution.py:25
  107.6 3.7 %collective-permute-start.3 = (bf16[2,64,9216]{2,1,0:T(8,128)(2,1)}, bf16[2,64,9216]{2,1,0:T(8,128)(2,1)}, u32[]{:S(2)}, u32[]{:S(2)}) collective-permute-start(bf16[2,64,9216]{2,1,0:T(8,128)(2,1)} %collective-permute-done), channel_id=1, source_target_pairs={{4,8},{5,9},{6,10},{7,11},{8,4},{9,5},{10,6},{11,7},{20,24},{21,25... | collective-permute-start | bytes 7077896 | tf_op jit(solution)/shard_map/ppermute | solution.py:25
  111.3 4.8 %all-to-all-start.1 = ((bf16[8,6,8,8192]{3,2,1,0:T(8,128)(2,1)}), bf16[8,6,8,8192]{3,2,1,0:T(8,128)(2,1)}, u32[]{:S(2)}, u32[]{:S(2)}) async-start(bf16[8,6,8,8192]{3,2,1,0:T(8,128)(2,1)} %bitcast.70), calls=%async_computation.1 | async-start | bytes 12582912 | tf_op jit(solution)/shard_map/all_to_all | solution.py:28
  116.0 3.0 %copy.16 = bf16[8,2,8,8192]{3,2,0,1:T(8,128)(2,1)} copy(bf16[8,2,8,8192]{3,2,1,0:T(8,128)(2,1)} %all-to-all-done) | data formatting | bytes 4194304 | tf_op jit(solution)/shard_map/all_to_all | solution.py:28
  119.1 1.3 collective-permute-start.4
  120.4 0.0 collective-permute-done.1
  120.4 7.3 %collective-permute-start.2 = (bf16[2,64,9216]{2,1,0:T(8,128)(2,1)}, bf16[2,64,9216]{2,1,0:T(8,128)(2,1)}, u32[]{:S(2)}, u32[]{:S(2)}) collective-permute-start(bf16[2,64,9216]{2,1,0:T(8,128)(2,1)} %collective-permute-done.1), channel_id=1, source_target_pairs={{4,0},{5,1},{6,2},{7,3},{8,12},{9,13},{10,14},{11,15},{20,16},{21,... | collective-permute-start | bytes 7077896 | tf_op jit(solution)/shard_map/ppermute | solution.py:25
  127.7 63.6 %collective-permute-done.4 = bf16[8,2,8,8192]{3,2,0,1:T(8,128)(2,1)} collective-permute-done((bf16[8,2,8,8192]{3,2,0,1:T(8,128)(2,1)}, bf16[8,2,8,8192]{3,2,0,1:T(8,128)(2,1)}, u32[]{:S(2)}, u32[]{:S(2)}) %collective-permute-start.4) | collective-permute-done | bytes 2097184 | tf_op jit(solution)/shard_map/ppermute | solution.py:25
  191.3 4.1 %collective-permute-done.3 = bf16[2,64,9216]{2,1,0:T(8,128)(2,1)} collective-permute-done((bf16[2,64,9216]{2,1,0:T(8,128)(2,1)}, bf16[2,64,9216]{2,1,0:T(8,128)(2,1)}, u32[]{:S(2)}, u32[]{:S(2)}) %collective-permute-start.3) | collective-permute-done | bytes 2359328 | tf_op jit(solution)/shard_map/ppermute | solution.py:25
  195.4 3.2 %fusion.11 = bf16[8,2,8,1024]{3,2,0,1:T(8,128)(2,1)S(1)} fusion(bf16[8,2,8,8192]{3,2,0,1:T(8,128)(2,1)} %collective-permute-done.4, bf16[2,64,9216]{2,1,0:T(8,128)(2,1)} %collective-permute-done.3), kind=kOutput, calls=%fused_computation.23 | convolution fusion | flops 151265280 | bytes 4718592 | tf_op jit(solution)/shard_map/sajr,arn->sajn/dot_general | solution.py:37
  198.6 1.3 collective-permute-start.5
  199.9 0.0 collective-permute-done.2
  199.9 3.6 %broadcast_select_fusion = bf16[2,64,9216]{2,1,0:T(8,128)(2,1)} fusion(bf16[2,64,9216]{2,1,0:T(8,128)(2,1)} %collective-permute-done.2, bf16[2,64,9216]{2,1,0:T(8,128)(2,1)} %collective-permute-done.1, pred[]{:T(512)S(6)} %or.3), kind=kLoop, calls=%fused_computation.10 | loop fusion | flops 1179648 | bytes 7077889 | tf_op jit(solution)/shard_map/jit(_where)/select_n | solution.py:111
  203.6 3.2 %fusion.10 = bf16[8,2,8,1024]{3,2,0,1:T(8,128)(2,1)S(1)} fusion(bf16[2,64,9216]{2,1,0:T(8,128)(2,1)} %collective-permute-done.3, bf16[8,2,8,8192]{3,2,1,0:T(8,128)(2,1)} %all-to-all-done), kind=kOutput, calls=%fused_computation.22 | convolution fusion | flops 151265280 | bytes 4718592 | tf_op jit(solution)/shard_map/sajr,arn->sajn/dot_general | solution.py:37
  206.8 10.2 %collective-permute-done.5 = bf16[8,2,8,1024]{3,2,0,1:T(8,128)(2,1)S(1)} collective-permute-done((bf16[8,2,8,1024]{3,2,0,1:T(8,128)(2,1)S(1)}, bf16[8,2,8,1024]{3,2,0,1:T(8,128)(2,1)S(1)}, u32[]{:S(2)}, u32[]{:S(2)}) %collective-permute-start.5) | collective-permute-done | bytes 262176 | tf_op jit(solution)/shard_map/ppermute | solution.py:25
  217.0 0.0 all-to-all-done.1
  217.0 6.5 %fusion.7 = bf16[8,6,8,1024]{3,2,0,1:T(8,128)(2,1)S(1)} fusion(bf16[8,6,8,8192]{3,2,1,0:T(8,128)(2,1)} %all-to-all-done.1, bf16[2,64,9216]{2,1,0:T(8,128)(2,1)} %broadcast_select_fusion, bf16[2,64,9216]{2,1,0:T(8,128)(2,1)} %collective-permute-done, bf16[2,64,1024]{2,1,0:T(8,128)(2,1)S(1)} %constant_dynamic-slice_fusion, ...), kind=kOutput, calls=%fused_computation.17 | convolution fusion | flops 482107392 | bytes 14155776 | tf_op jit(solution)/shard_map/sajr,arn->sajn/dot_general | solution.py:37
  223.4 0.1 pad_maximum_fusion.6
  223.6 1.1 copy.18
  224.6 5.9 %all-to-all-start.2 = ((bf16[8,8,8,1024]{3,2,1,0:T(8,128)(2,1)}), bf16[8,8,8,1024]{3,2,1,0:T(8,128)(2,1)S(1)}, u32[]{:S(2)}, u32[]{:S(2)}) async-start(bf16[8,8,8,1024]{3,2,1,0:T(8,128)(2,1)} %copy.18), calls=%async_computation.2 | async-start | bytes 2097152 | tf_op jit(solution)/shard_map/all_to_all | solution.py:28
  230.5 0.0 all-gather.2.cloned.1.call-done
  230.5 0.0 copy-start.1
  230.5 15.8 %fusion.99 = f32[512,1024]{1,0:T(8,128)} fusion(bf16[512,8192]{1,0:T(8,128)(2,1)} %param.6, bf16[8192,1024]{1,0:T(8,128)(2,1)} %all-gather.2.cloned.1.call-done), kind=kOutput, calls=%fused_computation.144 | convolution fusion | flops 8589934592 | bytes 27262976 | tf_op jit(solution)/shard_map/dot_general | solution.py:108
  246.4 0.0 all-to-all-done.2
  246.4 3.3 %add_convert_fusion = bf16[512,1024]{1,0:T(8,128)(2,1)} fusion(f32[512,1024]{1,0:T(8,128)} %fusion.99, bf16[512,1024]{1,0:T(8,128)(2,1)S(1)} %bitcast.71, s32[512]{0:T(512)S(1)} %get-tuple-element.12, s32[512]{0:T(512)S(1)} %get-tuple-element.11), kind=kOutput, calls=%fused_computation.12 | convolution fusion | flops 538181632 | bytes 4198400 | tf_op jit(solution)/shard_map/dot_general | solution.py:93
  249.7 0.0 copy-done.1
  (5 shorter events, 0.1 us)
Async XLA Ops:
  6.5 1.0 copy-start
  6.5 224.0 %all-gather.2.cloned.1.call-start = ((), (), s32[]{:S(2)}) async-start(), calls=%async_computation.3 | async-start | bytes 17825792 | tf_op jit(solution)/shard_map/all_gather | solution.py:108
  9.4 5.2 %copy-start.2 = (s32[512]{0:T(512)S(1)}, s32[512]{0:T(512)}, u32[]{:S(2)}) copy-start(s32[512]{0:T(512)} %param.10) | copy-start | bytes 6148
  9.4 5.2 %copy-start.3 = (s32[64]{0:T(128)S(1)}, s32[64]{0:T(128)}, u32[]{:S(2)}) copy-start(s32[64]{0:T(128)} %param.11) | copy-start | bytes 772
  11.0 109.4 %collective-permute-start.1 = (bf16[2,64,9216]{2,1,0:T(8,128)(2,1)}, bf16[2,64,9216]{2,1,0:T(8,128)(2,1)}, u32[]{:S(2)}, u32[]{:S(2)}) collective-permute-start(bf16[2,64,9216]{2,1,0:T(8,128)(2,1)} %pad_maximum_fusion.5), channel_id=1, source_target_pairs={{4,8},{5,9},{6,10},{7,11},{8,4},{9,5},{10,6},{11,7},{20,24},{21,25... | collective-permute-start | bytes 7077896 | tf_op jit(solution)/shard_map/ppermute | solution.py:25
  14.5 93.1 %collective-permute-start = (bf16[2,64,9216]{2,1,0:T(8,128)(2,1)}, bf16[2,64,9216]{2,1,0:T(8,128)(2,1)}, u32[]{:S(2)}, u32[]{:S(2)}) collective-permute-start(bf16[2,64,9216]{2,1,0:T(8,128)(2,1)} %pad_maximum_fusion.5), channel_id=1, source_target_pairs={{0,4},{1,5},{2,6},{3,7},{4,0},{5,1},{6,2},{7,3},{8,12},{9,13},{10,... | collective-permute-start | bytes 7077896 | tf_op jit(solution)/shard_map/ppermute | solution.py:25
  21.2 34.4 %all-to-all-start = ((bf16[8,2,8,8192]{3,2,1,0:T(8,128)(2,1)}), bf16[8,2,8,8192]{3,2,1,0:T(8,128)(2,1)}, u32[]{:S(2)}, u32[]{:S(2)}) async-start(bf16[8,2,8,8192]{3,2,1,0:T(8,128)(2,1)} %bitcast.69), calls=%async_computation | async-start | bytes 4194304 | tf_op jit(solution)/shard_map/all_to_all | solution.py:28
  107.6 87.9 %collective-permute-start.3 = (bf16[2,64,9216]{2,1,0:T(8,128)(2,1)}, bf16[2,64,9216]{2,1,0:T(8,128)(2,1)}, u32[]{:S(2)}, u32[]{:S(2)}) collective-permute-start(bf16[2,64,9216]{2,1,0:T(8,128)(2,1)} %collective-permute-done), channel_id=1, source_target_pairs={{4,8},{5,9},{6,10},{7,11},{8,4},{9,5},{10,6},{11,7},{20,24},{21,25... | collective-permute-start | bytes 7077896 | tf_op jit(solution)/shard_map/ppermute | solution.py:25
  111.3 105.7 %all-to-all-start.1 = ((bf16[8,6,8,8192]{3,2,1,0:T(8,128)(2,1)}), bf16[8,6,8,8192]{3,2,1,0:T(8,128)(2,1)}, u32[]{:S(2)}, u32[]{:S(2)}) async-start(bf16[8,6,8,8192]{3,2,1,0:T(8,128)(2,1)} %bitcast.70), calls=%async_computation.1 | async-start | bytes 12582912 | tf_op jit(solution)/shard_map/all_to_all | solution.py:28
  119.1 72.2 %collective-permute-start.4 = (bf16[8,2,8,8192]{3,2,0,1:T(8,128)(2,1)}, bf16[8,2,8,8192]{3,2,0,1:T(8,128)(2,1)}, u32[]{:S(2)}, u32[]{:S(2)}) collective-permute-start(bf16[8,2,8,8192]{3,2,0,1:T(8,128)(2,1)} %copy.16), channel_id=1, source_target_pairs={{0,4},{1,5},{2,6},{3,7},{12,8},{13,9},{14,10},{15,11},{16,20},{17,... | collective-permute-start | bytes 6291464 | tf_op jit(solution)/shard_map/ppermute | solution.py:25
  120.4 79.5 %collective-permute-start.2 = (bf16[2,64,9216]{2,1,0:T(8,128)(2,1)}, bf16[2,64,9216]{2,1,0:T(8,128)(2,1)}, u32[]{:S(2)}, u32[]{:S(2)}) collective-permute-start(bf16[2,64,9216]{2,1,0:T(8,128)(2,1)} %collective-permute-done.1), channel_id=1, source_target_pairs={{4,0},{5,1},{6,2},{7,3},{8,12},{9,13},{10,14},{11,15},{20,16},{21,... | collective-permute-start | bytes 7077896 | tf_op jit(solution)/shard_map/ppermute | solution.py:25
  198.6 18.3 %collective-permute-start.5 = (bf16[8,2,8,1024]{3,2,0,1:T(8,128)(2,1)S(1)}, bf16[8,2,8,1024]{3,2,0,1:T(8,128)(2,1)S(1)}, u32[]{:S(2)}, u32[]{:S(2)}) collective-permute-start(bf16[8,2,8,1024]{3,2,0,1:T(8,128)(2,1)S(1)} %fusion.11), channel_id=1, source_target_pairs={{4,0},{5,1},{6,2},{7,3},{8,12},{9,13},{10,14},{11,15},{20,16},{21,... | collective-permute-start | bytes 786440 | tf_op jit(solution)/shard_map/ppermute | solution.py:25
  224.6 21.7 %all-to-all-start.2 = ((bf16[8,8,8,1024]{3,2,1,0:T(8,128)(2,1)}), bf16[8,8,8,1024]{3,2,1,0:T(8,128)(2,1)S(1)}, u32[]{:S(2)}, u32[]{:S(2)}) async-start(bf16[8,8,8,1024]{3,2,1,0:T(8,128)(2,1)} %copy.18), calls=%async_computation.2 | async-start | bytes 2097152 | tf_op jit(solution)/shard_map/all_to_all | solution.py:28
  230.5 19.2 %copy-start.1 = (bf16[4,64,1024]{2,1,0:T(8,128)(2,1)S(1)}, bf16[4,64,1024]{2,1,0:T(8,128)(2,1)}, u32[]{:S(2)}) copy-start(bf16[4,64,1024]{2,1,0:T(8,128)(2,1)} %param.9) | copy-start | bytes 1572868
Sparse Core Ops, SparseCore 0:
  9.5 218.1 all-gather.1
